TPU v7x, 32 devices: a whole 2x2x4 slice. The times are simulated.
32 devices in a mesh: fsdp: 8 (over z, core), seq: 4 (over y, x).
Axes of the slice: x: 2, y: 2, z: 4, core: 2. Of those that a mesh axis runs over, the one named last changes fastest.
Arguments:
- inputs: bfloat16 [8, 1024, 1024], P('fsdp', 'seq'), may hold values from -6 to 6
- segments: int32 [8, 1024], P('fsdp'), may hold values from 0 to 1, as said below
- cotangent: bfloat16 [8, 1024, 1024], P('fsdp', 'seq'), may hold values from -6 to 6
- first_gain: bfloat16 [1024], P(('fsdp', 'seq')), may hold values from 0.5 to 1.5
- first_shift: bfloat16 [1024], P(('fsdp', 'seq')), may hold values from -2 to 2
- qkv_weight: bfloat16 [1024, 3072], P(('fsdp', 'seq')), may hold values from -0.1875 to 0.1875
- query_bias: bfloat16 [1024], P(('fsdp', 'seq')), may hold values from -3 to 3
- value_bias: bfloat16 [1024], P(('fsdp', 'seq')), may hold values from -3 to 3
- output_weight: bfloat16 [1024, 1024], P(('fsdp', 'seq')), may hold values from -1 to 1
- output_bias: bfloat16 [1024], P(('fsdp', 'seq')), may hold values from -3 to 3
- second_gain: bfloat16 [1024], P(('fsdp', 'seq')), may hold values from 0.5 to 1.5
- second_shift: bfloat16 [1024], P(('fsdp', 'seq')), may hold values from -2 to 2
- expand_weight: bfloat16 [1024, 4096], P(('fsdp', 'seq')), may hold values from -0.1875 to 0.1875
- expand_bias: bfloat16 [4096], P(('fsdp', 'seq')), may hold values from -3 to 3
- shrink_weight: bfloat16 [4096, 1024], P(('fsdp', 'seq')), may hold values from -0.09375 to 0.09375
- shrink_bias: bfloat16 [1024], P(('fsdp', 'seq')), may hold values from -3 to 3
Outputs:
- outputs: bfloat16 [8, 1024, 1024], P('fsdp', 'seq')
- input_grad: bfloat16 [8, 1024, 1024], P('fsdp', 'seq')
- first_gain_grad: float32 [1024], P(('fsdp', 'seq'))
- first_shift_grad: float32 [1024], P(('fsdp', 'seq'))
- qkv_weight_grad: float32 [1024, 3072], P(('fsdp', 'seq'))
- query_bias_grad: float32 [1024], P(('fsdp', 'seq'))
- value_bias_grad: float32 [1024], P(('fsdp', 'seq'))
- output_weight_grad: float32 [1024, 1024], P(('fsdp', 'seq'))
- output_bias_grad: float32 [1024], P(('fsdp', 'seq'))
- second_gain_grad: float32 [1024], P(('fsdp', 'seq'))
- second_shift_grad: float32 [1024], P(('fsdp', 'seq'))
- expand_weight_grad: float32 [1024, 4096], P(('fsdp', 'seq'))
- expand_bias_grad: float32 [4096], P(('fsdp', 'seq'))
- shrink_weight_grad: float32 [4096, 1024], P(('fsdp', 'seq'))
- shrink_bias_grad: float32 [1024], P(('fsdp', 'seq'))
Inputs may be any that keep to these rules, and one draw needn't show every extreme that they name: `segments`: along each sequence the numbers start at 0 and rise by 0 or 1 from one token to the next; every sequence holds exactly 2 documents; in each aligned block of 1 sequence, the first document of one sequence covers all but the last 256 tokens or fewer.
All inputs are finite; a program needn't handle non-finite values.
Results may differ from a plain program's by a relative error of at most 0.012.
Values may be sent and summed in bfloat16 or wider, within the bound.
A program may use at most 256 MiB of HBM per device.

v0:
```python
import jax
import jax.numpy as jnp
from jax import lax
from jax.sharding import PartitionSpec as P

HEAD_DIM = 64


def layer_norm(values, gain, shift):
    centre = values - jnp.mean(values, axis=-1, keepdims=True)
    spread = jnp.mean(centre * centre, axis=-1, keepdims=True)
    return centre * lax.rsqrt(spread + 1e-05) * gain + shift


def gelu_tanh(values):
    return (
        0.5
        * values
        * (1.0 + jnp.tanh(0.7978845608028654 * (values + 0.044715 * values * values * values)))
    )


def rows_product(left, right):
    return jnp.dot(left, right, preferred_element_type=jnp.float32)


def weight_grad(left, right):
    return lax.dot_general(
        left, right, (((0,), (0,)), ((), ())), preferred_element_type=jnp.float32
    )


def input_grad(left, right):
    return lax.dot_general(
        left, right, (((1,), (1,)), ((), ())), preferred_element_type=jnp.float32
    )


def column_sum(values):
    return jnp.sum(values.astype(jnp.float32), axis=0)


def masked_scores(queries, keys, allowed):
    scores = (
        jnp.einsum("bqhd,bkhd->bhqk", queries, keys, preferred_element_type=jnp.float32) * 0.125
    )
    return jnp.where(allowed, scores, -1e30)


def local(
    inputs,
    segments,
    cotangent,
    first_gain,
    first_shift,
    qkv_weight,
    query_bias,
    value_bias,
    output_weight,
    output_bias,
    second_gain,
    second_shift,
    expand_weight,
    expand_bias,
    shrink_weight,
    shrink_bias,
):
    forward_set = (
        lax.all_gather(first_gain, ("fsdp", "seq"), axis=0, tiled=True),
        lax.all_gather(first_shift, ("fsdp", "seq"), axis=0, tiled=True),
        lax.all_gather(qkv_weight, ("fsdp", "seq"), axis=0, tiled=True),
        lax.all_gather(query_bias, ("fsdp", "seq"), axis=0, tiled=True),
        lax.all_gather(value_bias, ("fsdp", "seq"), axis=0, tiled=True),
        lax.all_gather(output_weight, ("fsdp", "seq"), axis=0, tiled=True),
        lax.all_gather(output_bias, ("fsdp", "seq"), axis=0, tiled=True),
        lax.all_gather(second_gain, ("fsdp", "seq"), axis=0, tiled=True),
        lax.all_gather(second_shift, ("fsdp", "seq"), axis=0, tiled=True),
        lax.all_gather(expand_weight, ("fsdp", "seq"), axis=0, tiled=True),
        lax.all_gather(expand_bias, ("fsdp", "seq"), axis=0, tiled=True),
        lax.all_gather(shrink_weight, ("fsdp", "seq"), axis=0, tiled=True),
        lax.all_gather(shrink_bias, ("fsdp", "seq"), axis=0, tiled=True),
    )
    seqs, group, width = inputs.shape
    length = segments.shape[1]
    heads = width // HEAD_DIM
    rows = seqs * group
    gain_first = forward_set[0].astype(jnp.float32)
    shift_first = forward_set[1].astype(jnp.float32)
    gain_second = forward_set[7].astype(jnp.float32)
    shift_second = forward_set[8].astype(jnp.float32)
    tokens = inputs.reshape(rows, width).astype(jnp.float32)
    acts_first = layer_norm(tokens, gain_first, shift_first).astype(jnp.bfloat16)
    joined = rows_product(acts_first, forward_set[2])
    query_rows = (joined[:, :width] + forward_set[3].astype(jnp.float32)).astype(jnp.bfloat16)
    key_local = joined[:, width : 2 * width].astype(jnp.bfloat16).reshape(seqs, group, width)
    value_local = (
        (joined[:, 2 * width :] + forward_set[4].astype(jnp.float32))
        .astype(jnp.bfloat16)
        .reshape(seqs, group, width)
    )
    key_all, value_all = (
        lax.all_gather(key_local, "seq", axis=1, tiled=True),
        lax.all_gather(value_local, "seq", axis=1, tiled=True),
    )
    first_place = lax.axis_index("seq") * group
    query_segment = lax.dynamic_slice_in_dim(segments, first_place, group, 1)
    query_place = first_place + jnp.arange(group)
    key_place = jnp.arange(length)
    causal = key_place[None, :] <= query_place[:, None]
    allowed = (causal[None] & (query_segment[:, :, None] == segments[:, None, :]))[:, None]
    query_heads = query_rows.reshape(seqs, group, heads, HEAD_DIM)
    scores = masked_scores(query_heads, key_all.reshape(seqs, length, heads, HEAD_DIM), allowed)
    largest = jnp.max(scores, axis=-1, keepdims=True)
    expon = jnp.exp(scores - largest)
    total = jnp.sum(expon, axis=-1, keepdims=True)
    probs = (expon / total).astype(jnp.bfloat16)
    mixed = jnp.einsum(
        "bhqk,bkhd->bqhd",
        probs,
        value_all.reshape(seqs, length, heads, HEAD_DIM),
        preferred_element_type=jnp.float32,
    )
    mixed = mixed.reshape(rows, width).astype(jnp.bfloat16)
    middle = tokens + rows_product(mixed, forward_set[5]) + forward_set[6].astype(jnp.float32)
    acts_second = layer_norm(middle, gain_second, shift_second).astype(jnp.bfloat16)
    hidden_pre = rows_product(acts_second, forward_set[9]) + forward_set[10].astype(jnp.float32)
    acts_third = gelu_tanh(hidden_pre).astype(jnp.bfloat16)
    result = (
        middle + rows_product(acts_third, forward_set[11]) + forward_set[12].astype(jnp.float32)
    )
    outputs = result.astype(jnp.bfloat16).reshape(seqs, group, width)
    back_set = (
        lax.all_gather(first_gain, ("fsdp", "seq"), axis=0, tiled=True),
        lax.all_gather(first_shift, ("fsdp", "seq"), axis=0, tiled=True),
        lax.all_gather(qkv_weight, ("fsdp", "seq"), axis=0, tiled=True),
        lax.all_gather(query_bias, ("fsdp", "seq"), axis=0, tiled=True),
        lax.all_gather(value_bias, ("fsdp", "seq"), axis=0, tiled=True),
        lax.all_gather(output_weight, ("fsdp", "seq"), axis=0, tiled=True),
        lax.all_gather(output_bias, ("fsdp", "seq"), axis=0, tiled=True),
        lax.all_gather(second_gain, ("fsdp", "seq"), axis=0, tiled=True),
        lax.all_gather(second_shift, ("fsdp", "seq"), axis=0, tiled=True),
        lax.all_gather(expand_weight, ("fsdp", "seq"), axis=0, tiled=True),
        lax.all_gather(expand_bias, ("fsdp", "seq"), axis=0, tiled=True),
        lax.all_gather(shrink_weight, ("fsdp", "seq"), axis=0, tiled=True),
        lax.all_gather(shrink_bias, ("fsdp", "seq"), axis=0, tiled=True),
    )
    grad_out = cotangent.reshape(rows, width)
    grad_shrink = weight_grad(acts_third, grad_out)
    grad_shrink_bias = column_sum(grad_out)
    grad_hidden = input_grad(grad_out, back_set[11])
    gelu_value, gelu_pull = jax.vjp(gelu_tanh, hidden_pre)
    grad_pre = gelu_pull(grad_hidden)[0].astype(jnp.bfloat16)
    grad_expand = weight_grad(acts_second, grad_pre)
    grad_expand_bias = column_sum(grad_pre)
    grad_acts_second = input_grad(grad_pre, back_set[9])
    norm_value, second_pull = jax.vjp(
        layer_norm, middle, back_set[7].astype(jnp.float32), back_set[8].astype(jnp.float32)
    )
    grad_middle_norm, grad_gain_second, grad_shift_second = second_pull(grad_acts_second)
    grad_middle = grad_out.astype(jnp.float32) + grad_middle_norm
    grad_branch = grad_middle.astype(jnp.bfloat16)
    grad_output = weight_grad(mixed, grad_branch)
    grad_output_bias = column_sum(grad_branch)
    grad_mixed = (
        input_grad(grad_branch, back_set[5])
        .astype(jnp.bfloat16)
        .reshape(seqs, group, heads, HEAD_DIM)
    )
    key_back, value_back = (
        lax.all_gather(key_local, "seq", axis=1, tiled=True),
        lax.all_gather(value_local, "seq", axis=1, tiled=True),
    )
    key_heads = key_back.reshape(seqs, length, heads, HEAD_DIM)
    value_heads = value_back.reshape(seqs, length, heads, HEAD_DIM)
    scores_again = masked_scores(query_heads, key_heads, allowed)
    probs_again = jnp.exp(scores_again - largest) / total
    grad_probs = jnp.einsum(
        "bqhd,bkhd->bhqk", grad_mixed, value_heads, preferred_element_type=jnp.float32
    )
    centred = jnp.sum(probs_again * grad_probs, axis=-1, keepdims=True)
    grad_scores = (probs_again * (grad_probs - centred)).astype(jnp.bfloat16)
    grad_query = (
        jnp.einsum("bhqk,bkhd->bqhd", grad_scores, key_heads, preferred_element_type=jnp.float32)
        * 0.125
    )
    key_terms = (
        jnp.einsum("bhqk,bqhd->bkhd", grad_scores, query_heads, preferred_element_type=jnp.float32)
        * 0.125
    )
    value_terms = jnp.einsum(
        "bhqk,bqhd->bkhd",
        probs_again.astype(jnp.bfloat16),
        grad_mixed,
        preferred_element_type=jnp.float32,
    )
    grad_key, grad_value = (
        lax.psum_scatter(
            key_terms.reshape(seqs, length, width).astype(jnp.bfloat16),
            "seq",
            scatter_dimension=1,
            tiled=True,
        ).astype(jnp.float32),
        lax.psum_scatter(
            value_terms.reshape(seqs, length, width).astype(jnp.bfloat16),
            "seq",
            scatter_dimension=1,
            tiled=True,
        ).astype(jnp.float32),
    )
    grad_joined = jnp.concatenate(
        [
            grad_query.reshape(rows, width),
            grad_key.reshape(rows, width),
            grad_value.reshape(rows, width),
        ],
        axis=1,
    ).astype(jnp.bfloat16)
    grad_qkv = weight_grad(acts_first, grad_joined)
    grad_query_bias = column_sum(grad_joined[:, :width])
    grad_value_bias = column_sum(grad_joined[:, 2 * width :])
    grad_acts_first = input_grad(grad_joined, back_set[2])
    first_value, first_pull = jax.vjp(
        layer_norm, tokens, back_set[0].astype(jnp.float32), back_set[1].astype(jnp.float32)
    )
    grad_tokens_norm, grad_gain_first, grad_shift_first = first_pull(grad_acts_first)
    grad_inputs = (grad_middle + grad_tokens_norm).astype(jnp.bfloat16).reshape(seqs, group, width)
    owned = (
        lax.psum_scatter(grad_gain_first, ("fsdp", "seq"), scatter_dimension=0, tiled=True),
        lax.psum_scatter(grad_shift_first, ("fsdp", "seq"), scatter_dimension=0, tiled=True),
        lax.psum_scatter(grad_qkv, ("fsdp", "seq"), scatter_dimension=0, tiled=True),
        lax.psum_scatter(grad_query_bias, ("fsdp", "seq"), scatter_dimension=0, tiled=True),
        lax.psum_scatter(grad_value_bias, ("fsdp", "seq"), scatter_dimension=0, tiled=True),
        lax.psum_scatter(grad_output, ("fsdp", "seq"), scatter_dimension=0, tiled=True),
        lax.psum_scatter(grad_output_bias, ("fsdp", "seq"), scatter_dimension=0, tiled=True),
        lax.psum_scatter(grad_gain_second, ("fsdp", "seq"), scatter_dimension=0, tiled=True),
        lax.psum_scatter(grad_shift_second, ("fsdp", "seq"), scatter_dimension=0, tiled=True),
        lax.psum_scatter(grad_expand, ("fsdp", "seq"), scatter_dimension=0, tiled=True),
        lax.psum_scatter(grad_expand_bias, ("fsdp", "seq"), scatter_dimension=0, tiled=True),
        lax.psum_scatter(grad_shrink, ("fsdp", "seq"), scatter_dimension=0, tiled=True),
        lax.psum_scatter(grad_shrink_bias, ("fsdp", "seq"), scatter_dimension=0, tiled=True),
    )
    return (outputs, grad_inputs) + tuple(owned)


def solution(mesh):
    placed = (
        P("fsdp", "seq", None),
        P("fsdp", None),
        P("fsdp", "seq", None),
        P(("fsdp", "seq")),
        P(("fsdp", "seq")),
        P(("fsdp", "seq"), None),
        P(("fsdp", "seq")),
        P(("fsdp", "seq")),
        P(("fsdp", "seq"), None),
        P(("fsdp", "seq")),
        P(("fsdp", "seq")),
        P(("fsdp", "seq")),
        P(("fsdp", "seq"), None),
        P(("fsdp", "seq")),
        P(("fsdp", "seq"), None),
        P(("fsdp", "seq")),
    )
    return jax.shard_map(
        local,
        mesh=mesh,
        in_specs=placed,
        out_specs=(
            P("fsdp", "seq", None),
            P("fsdp", "seq", None),
            P(("fsdp", "seq")),
            P(("fsdp", "seq")),
            P(("fsdp", "seq"), None),
            P(("fsdp", "seq")),
            P(("fsdp", "seq")),
            P(("fsdp", "seq"), None),
            P(("fsdp", "seq")),
            P(("fsdp", "seq")),
            P(("fsdp", "seq")),
            P(("fsdp", "seq"), None),
            P(("fsdp", "seq")),
            P(("fsdp", "seq"), None),
            P(("fsdp", "seq")),
        ),
        check_vma=False,
    )
```

profile of v0, /device:TPU:0, one launch (start us, length us, event | category | flops | bytes accessed | tf_op | source)
XLA Modules:
  0.0 1510.2 jit_solution(7648427285675508873)
XLA Ops:
  14.7 42.7 %all-reduce.18 = (bf16[1024]{0:T(1024)(128)(2,1)S(1)}, bf16[1024]{0:T(1024)(128)(2,1)S(1)}, bf16[1024]{0:T(1024)(128)(2,1)S(1)}, bf16[1024]{0:T(1024)(128)(2,1)S...) all-reduce(bf16[1024]{0:T(1024)(128)(2,1)S(1)} %dynamic-update-slic, ...), channel_id=1, replica_groups=mesh['fsdp'=8,'seq'=4] {'fsdp','seq'}, use_global_device_ids=true, to_apply=%add.1 | all-reduce | flops 8192 | bytes 32768
  60.6 22.8 %all-gather.10.cloned.1.call-done = bf16[1024,3072]{1,0:T(8,128)(2,1)} async-done(((bf16[32,3072]{1,0:T(8,128)(2,1)}), bf16[1024,3072]{1,0:T(8,128)(2,1)}) %all-gather.10.cloned.1.call-update) | async-done | bytes 6291472 | tf_op jit(solution)/shard_map/all_gather | solution.py:71
  83.4 4.9 fusion.60
  92.3 65.7 %all-gather.2 = bf16[32,1,128]{2,1,0:T(2,128)(2,1)S(1)} all-gather(bf16[1,1,128]{2,1,0:T(2,128)(2,1)S(1)} %bitcast.132), channel_id=1, replica_groups=mesh['fsdp'=8,'seq'=4] {'fsdp','seq'}, dimensions={0}, use_global_device_ids=true | all-gather | bytes 8448 | tf_op jit(solution)/shard_map/all_gather | solution.py:79
  159.7 4.1 copy.43
  163.8 2.9 copy.45
  166.7 9.4 fusion.67
  176.1 9.2 fusion.29
  185.3 35.4 %all-gather.12.cloned.1.call-done = bf16[1024,1024]{1,0:T(8,128)(2,1)} async-done(((bf16[32,1024]{1,0:T(8,128)(2,1)}), bf16[1024,1024]{1,0:T(8,128)(2,1)}) %all-gather.12.cloned.1.call-update) | async-done | bytes 2097168 | tf_op jit(solution)/shard_map/all_gather | solution.py:74
  220.7 2.4 fusion.68
  223.4 76.5 %all-gather.14.cloned.1.call-done = bf16[1024,4096]{1,0:T(8,128)(2,1)} async-done(((bf16[32,4096]{1,0:T(8,128)(2,1)}), bf16[1024,4096]{1,0:T(8,128)(2,1)}) %all-gather.14.cloned.1.call-update) | async-done | bytes 8388624 | tf_op jit(solution)/shard_map/all_gather | solution.py:78
  299.8 8.0 convolution_add_fusion
  307.8 70.9 %all-gather.16.cloned.1.call-done = bf16[4096,1024]{1,0:T(8,128)(2,1)} async-done(((bf16[128,1024]{1,0:T(8,128)(2,1)}), bf16[4096,1024]{1,0:T(8,128)(2,1)}) %all-gather.16.cloned.1.call-update) | async-done | bytes 8388624 | tf_op jit(solution)/shard_map/all_gather | solution.py:80
  378.7 8.9 convert_reduce_fusion
  387.7 2.7 multiply_reduce_fusion.1
  395.6 9.3 fusion.15
  404.9 12.2 multiply_reduce_fusion
  417.1 12.0 multiply_convert_fusion
  429.2 3.4 multiply_convert_fusion.1
  433.2 3.9 fusion.69
  437.6 7.5 fusion.28
  445.1 32.2 %reduce-scatter.7.cloned.1.call-done = bf16[1,256,1024]{1,2,0:T(8,128)(2,1)} async-done(((bf16[1,1024,1024]{1,2,0:T(8,128)(2,1)}), bf16[1,256,1024]{1,2,0:T(8,128)(2,1)}) %reduce-scatter.7.cloned.1.call-update) | async-done | bytes 524304 | tf_op jit(solution)/shard_map/reduce_scatter | solution.py:197
  477.3 7.9 fusion.44
  485.3 10.8 fusion.47
  496.3 9.8 fusion.63
  508.1 8.4 fusion.32
  516.7 4.8 fusion.64
  523.4 41.1 %all-reduce.17 = (f32[1024]{0:T(1024)S(1)}, f32[1024]{0:T(1024)S(1)}, f32[1024]{0:T(1024)S(1)}, f32[1024]{0:T(1024)S(1)}, f32[1024]{0:T(1024)S(1)}, /*index=5*/f...) all-reduce(f32[1024]{0:T(1024)S(1)} %get-tuple-element.17, ...), channel_id=6, replica_groups=mesh['fsdp'=8,'seq'=4] {'fsdp','seq'}, use_global_device_ids=true, to_apply=%region_14.15.clone | all-reduce | flops 12288 | bytes 98304
  569.8 52.2 %reduce-scatter.13.cloned.1.call-done = f32[32,1024]{1,0:T(8,128)} async-done(((f32[1024,1024]{1,0:T(8,128)}), f32[32,1024]{1,0:T(8,128)}) %reduce-scatter.13.cloned.1.call-update) | async-done | bytes 131088 | tf_op jit(solution)/shard_map/reduce_scatter | solution.py:233
  622.0 159.5 %reduce-scatter.11.cloned.1.call-done = f32[32,3072]{1,0:T(8,128)} async-done(((f32[1024,3072]{1,0:T(8,128)}), f32[32,3072]{1,0:T(8,128)}) %reduce-scatter.11.cloned.1.call-update) | async-done | bytes 393232 | tf_op jit(solution)/shard_map/reduce_scatter | solution.py:230
  781.6 359.8 %reduce-scatter.17.cloned.1.call-done = f32[128,1024]{1,0:T(8,128)} async-done(((f32[4096,1024]{1,0:T(8,128)}), f32[128,1024]{1,0:T(8,128)}) %reduce-scatter.17.cloned.1.call-update) | async-done | bytes 524304 | tf_op jit(solution)/shard_map/reduce_scatter | solution.py:239
  1141.3 361.9 %reduce-scatter.15.cloned.1.call-done = f32[32,4096]{1,0:T(8,128)} async-done(((f32[1024,4096]{1,0:T(8,128)}), f32[32,4096]{1,0:T(8,128)}) %reduce-scatter.15.cloned.1.call-update) | async-done | bytes 524304 | tf_op jit(solution)/shard_map/reduce_scatter | solution.py:237
  (124 shorter events, 32.2 us)
Async XLA Ops:
  7.2 76.2 %all-gather.10.cloned.1.call-start = ((), (), s32[]{:S(2)}) async-start(), calls=%async_computation.6 | async-start | bytes 6488064 | tf_op jit(solution)/shard_map/all_gather | solution.py:71
  7.9 151.8 %all-gather.18.cloned.1.call-start = ((), (), s32[]{:S(2)}) async-start(), calls=%async_computation.16 | async-start | bytes 2621440 | tf_op jit(solution)/shard_map/all_gather | solution.py:103
  60.1 0.5 copy-start.13
  88.3 4.0 copy-start.17
  88.3 69.8 %copy-start.15 = (s32[1,1024]{1,0:T(1,128)S(1)}, s32[1,1024]{1,0:T(1,128)}, u32[]{:S(2)}) copy-start(s32[1,1024]{1,0:T(1,128)} %param.17) | copy-start | bytes 12292
  89.6 74.2 %all-gather.20.cloned.1.call-start = ((), (), s32[]{:S(2)}) async-start(), calls=%async_computation.17 | async-start | bytes 2621440 | tf_op jit(solution)/shard_map/all_gather | solution.py:102
  90.5 130.2 %all-gather.12.cloned.1.call-start = ((), (), s32[]{:S(2)}) async-start(), calls=%async_computation.7 | async-start | bytes 2162688 | tf_op jit(solution)/shard_map/all_gather | solution.py:74
  91.1 208.7 %all-gather.14.cloned.1.call-start = ((), (), s32[]{:S(2)}) async-start(), calls=%async_computation.8 | async-start | bytes 8650752 | tf_op jit(solution)/shard_map/all_gather | solution.py:78
  91.7 287.1 %all-gather.16.cloned.1.call-start = ((), (), s32[]{:S(2)}) async-start(), calls=%async_computation.9 | async-start | bytes 8650752 | tf_op jit(solution)/shard_map/all_gather | solution.py:80
  92.2 352.8 %reduce-scatter.9.cloned.1.call-start = ((), (), s32[]{:S(2)}) async-start(), calls=%async_computation.11 | async-start | bytes 2621440 | tf_op jit(solution)/shard_map/reduce_scatter | solution.py:203
  159.7 7.0 copy-start.6
  166.7 9.4 copy-start.2
  176.1 44.6 %copy-start.1 = (bf16[1,256,1024]{2,1,0:T(8,128)(2,1)S(1)}, bf16[1,256,1024]{2,1,0:T(8,128)(2,1)}, u32[]{:S(2)}) copy-start(bf16[1,256,1024]{2,1,0:T(8,128)(2,1)} %param.16) | copy-start | bytes 1572868
  185.3 122.5 %copy-start.5 = (bf16[16,64,256]{2,1,0:T(8,128)(2,1)}, bf16[16,64,256]{2,1,0:T(8,128)(2,1)S(1)}, u32[]{:S(2)}) copy-start(bf16[16,64,256]{2,1,0:T(8,128)(2,1)S(1)} %fusion.29) | copy-start | bytes 1572868
  299.8 78.9 %copy-start.3 = (bf16[1,256,1024]{2,1,0:T(8,128)(2,1)S(1)}, bf16[1,256,1024]{2,1,0:T(8,128)(2,1)}, u32[]{:S(2)}) copy-start(bf16[1,256,1024]{2,1,0:T(8,128)(2,1)} %param.18) | copy-start | bytes 1572868
  378.7 9.0 copy-start.18
  387.7 2.7 copy-start.11
  390.4 1.6 copy-start.8
  391.1 0.8 copy-start.10
  404.9 72.4 %reduce-scatter.7.cloned.1.call-start = ((), (), s32[]{:S(2)}) async-start(), calls=%async_computation.10 | async-start | bytes 2621440 | tf_op jit(solution)/shard_map/reduce_scatter | solution.py:197
  417.1 12.0 copy-start.7
  429.2 3.9 copy-start
  433.1 188.9 %reduce-scatter.13.cloned.1.call-start = ((), (), s32[]{:S(2)}) async-start(), calls=%async_computation.13 | async-start | bytes 4325376 | tf_op jit(solution)/shard_map/reduce_scatter | solution.py:233
  437.1 344.5 %reduce-scatter.11.cloned.1.call-start = ((), (), s32[]{:S(2)}) async-start(), calls=%async_computation.12 | async-start | bytes 12976128 | tf_op jit(solution)/shard_map/reduce_scatter | solution.py:230
  485.2 656.1 %reduce-scatter.17.cloned.1.call-start = ((), (), s32[]{:S(2)}) async-start(), calls=%async_computation.15 | async-start | bytes 17301504 | tf_op jit(solution)/shard_map/reduce_scatter | solution.py:239
  496.1 1007.1 %reduce-scatter.15.cloned.1.call-start = ((), (), s32[]{:S(2)}) async-start(), calls=%async_computation.14 | async-start | bytes 17301504 | tf_op jit(solution)/shard_map/reduce_scatter | solution.py:237
  506.2 0.7 copy-start.16
  508.1 8.4 copy-start.9
  508.1 8.6 copy-start.4
  508.1 8.6 copy-start.12
  516.7 4.8 copy-start.14
Sparse Core Ops, SparseCore 0:
  10.9 72.4 all-gather.9
  89.7 33.9 all-gather.17
  126.1 35.3 all-gather.19
  164.3 56.3 all-gather.11
  223.4 76.3 all-gather.13
  302.6 76.1 all-gather.15
  405.0 33.7 reduce-scatter.8
  442.1 35.1 reduce-scatter.6
  480.2 141.8 reduce-scatter.12
  628.5 153.0 reduce-scatter.10
  784.6 356.7 reduce-scatter.16
  1144.2 358.9 reduce-scatter.14
where the time goes:
time: 1520 us; the launch traced here: 1510 us
  waiting for transfers between devices  1170 us (77%)
  blocking collectives  149 us (10%)
  matrix products  125 us (8%)
  local copies, waits for them, and re-layouts  25.7 us (2%)
  other arithmetic  20.5 us (1%)
    reduce_scatter x1, waiting for transfers between devices, local(): lax.psum_scatter(grad_expand, ('fsdp', 'seq'), scatter_dimension=0, tiled...  362 us
    reduce_scatter x1, waiting for transfers between devices, local(): lax.psum_scatter(grad_shrink, ('fsdp', 'seq'), scatter_dimension=0, tiled...  360 us
    reduce_scatter x1, waiting for transfers between devices, local(): lax.psum_scatter(grad_qkv, ('fsdp', 'seq'), scatter_dimension=0, tiled=True)  160 us
    unnamed x2, blocking collectives  83.8 us
    all_gather x1, waiting for transfers between devices, local(): lax.all_gather(expand_weight, ('fsdp', 'seq'), axis=0, tiled=True)  76.5 us
    all_gather x1, waiting for transfers between devices, local(): lax.all_gather(shrink_weight, ('fsdp', 'seq'), axis=0, tiled=True)  70.9 us
    all_gather x1, blocking collectives, local(): lax.all_gather(expand_bias, ('fsdp', 'seq'), axis=0, tiled=True)  65.7 us
    reduce_scatter x1, waiting for transfers between devices, local(): lax.psum_scatter(grad_output, ('fsdp', 'seq'), scatter_dimension=0, tiled...  52.2 us
  transfers between devices with their start and end apart: 12, of which 9 were waited for; matrix products, arithmetic and copies ran while one was open for 9% of the time, Pallas kernels for 0%

commit v1 on v0

--- a/solution.py
+++ b/solution.py
@@ -1,9 +1,405 @@
+import functools
+import math
+
 import jax
 import jax.numpy as jnp
 from jax import lax
+from jax.experimental import pallas as pl
+from jax.experimental.pallas import tpu as pltpu
 from jax.sharding import PartitionSpec as P
 
 HEAD_DIM = 64
+
+BLOCK_ROWS = 32
+BLOCK_COLUMNS = 1024
+MESH = pl.DeviceIdType.MESH
+
+
+def lattice(group_count, place_count):
+    side = math.isqrt(place_count)
+    return {"z": group_count // 2, "core": 2, "y": place_count // side, "x": side}
+
+
+def here(sizes):
+    group, place = lax.axis_index("fsdp"), lax.axis_index("seq")
+    return {
+        "z": group // 2,
+        "core": lax.rem(group, 2),
+        "y": place // sizes["x"],
+        "x": lax.rem(place, sizes["x"]),
+    }
+
+
+def moved(me, sizes, dim, step):
+    other = dict(me)
+    other[dim] = lax.rem(me[dim] + step + sizes[dim], sizes[dim])
+    return other
+
+
+def device_of(at, sizes):
+    return {"fsdp": at["z"] * 2 + at["core"], "seq": at["y"] * sizes["x"] + at["x"]}
+
+
+def greet(me, sizes, dims):
+    barrier = pltpu.get_barrier_semaphore()
+    count = 0
+    for dim in dims:
+        for step in range(1, sizes[dim]):
+            pl.semaphore_signal(
+                barrier,
+                inc=1,
+                device_id=device_of(moved(me, sizes, dim, step), sizes),
+                device_id_type=MESH,
+            )
+            count += 1
+    pl.semaphore_wait(barrier, count)
+
+
+def pieces_of(shapes, rows_most, columns_most):
+    pieces = []
+    for item, (rows, columns) in enumerate(shapes):
+        high, wide = min(rows, rows_most), min(columns, columns_most)
+        if rows % high:
+            high = rows
+        if columns % wide:
+            wide = columns
+        for row in range(0, rows, high):
+            for column in range(0, columns, wide):
+                pieces.append((item, row, column, high, wide))
+    return pieces
+
+
+def slots_of(dims, sizes):
+    return {
+        dim: sum(sizes[other] - 1 for other in dims[: at]) for at, dim in enumerate(dims)
+    }, sum(sizes[dim] - 1 for dim in dims)
+
+
+def gather_kernel(dims, sizes, pieces, count, *refs):
+    ins, outs = refs[:count], refs[count : 2 * count]
+    send_sem, recv_sem, own_sem = refs[2 * count :]
+    me = here(sizes)
+    greet(me, sizes, dims)
+    slot, _ = slots_of(dims, sizes)
+    own = [
+        pltpu.make_async_copy(
+            ins[item], outs[item].at[tuple(me[dim] for dim in dims)], own_sem.at[item]
+        )
+        for item in range(count)
+    ]
+    for copy in own:
+        copy.start()
+    own_waited = set()
+
+    def order_of(number):
+        across = ("x", "y") if number % 2 == 0 else ("y", "x")
+        return [dim for dim in ("z",) + across + ("core",) if dim in dims]
+
+    def region(number, stage, at):
+        item, row, column, high, wide = pieces[number]
+        done = order_of(number)[:stage]
+        index = tuple(slice(None) if dim in done else at[dim] for dim in dims)
+        return outs[item].at[index + (pl.ds(row, high), pl.ds(column, wide))]
+
+    def copy_of(number, stage, step, source, target, device):
+        place = slot[order_of(number)[stage]] + step - 1
+        return pltpu.make_async_remote_copy(
+            src_ref=source,
+            dst_ref=target,
+            send_sem=send_sem.at[number, place],
+            recv_sem=recv_sem.at[number, place],
+            device_id=device_of(device, sizes),
+            device_id_type=MESH,
+        )
+
+    def receive(number, stage):
+        dim = order_of(number)[stage]
+        for step in range(1, sizes[dim]):
+            giver = moved(me, sizes, dim, -step)
+            landed = region(number, stage, giver)
+            copy_of(number, stage, step, landed, landed, giver).wait_recv()
+
+    sent = []
+    depth = len(dims)
+    for tick in range(len(pieces) + depth):
+        for stage in range(depth, -1, -1):
+            number = tick - stage
+            if not 0 <= number < len(pieces):
+                continue
+            item, row, column, high, wide = pieces[number]
+            if stage > 0:
+                receive(number, stage - 1)
+            if stage == depth:
+                continue
+            if stage == 1 and item not in own_waited:
+                own[item].wait()
+                own_waited.add(item)
+            dim = order_of(number)[stage]
+            target = region(number, stage, me)
+            source = target
+            if stage == 0:
+                source = ins[item].at[pl.ds(row, high), pl.ds(column, wide)]
+            for step in range(1, sizes[dim]):
+                copy = copy_of(
+                    number, stage, step, source, target, moved(me, sizes, dim, step)
+                )
+                copy.start()
+                sent.append(copy)
+    for copy in sent:
+        copy.wait_send()
+    for item in range(count):
+        if item not in own_waited:
+            own[item].wait()
+
+
+def gather_blocks(shards, dims, sizes, pieces, identity):
+    count = len(shards)
+    _, total = slots_of(dims, sizes)
+    front = tuple(sizes[dim] for dim in dims)
+    return pl.pallas_call(
+        functools.partial(gather_kernel, dims, sizes, pieces, count),
+        out_shape=[jax.ShapeDtypeStruct(front + s.shape, s.dtype) for s in shards],
+        in_specs=[pl.BlockSpec(memory_space=pl.ANY)] * count,
+        out_specs=[pl.BlockSpec(memory_space=pl.ANY)] * count,
+        scratch_shapes=[
+            pltpu.SemaphoreType.DMA((len(pieces), total)),
+            pltpu.SemaphoreType.DMA((len(pieces), total)),
+            pltpu.SemaphoreType.DMA((count,)),
+        ],
+        compiler_params=pltpu.CompilerParams(collective_id=identity, has_side_effects=True),
+    )(*shards)
+
+
+def scatter_plan(number, dims):
+    across = ("x", "y") if number % 2 == 0 else ("y", "x")
+    return [dim for dim in ("core",) + across + ("z",) if dim in dims]
+
+
+def landing_shape(number, stage, dims, sizes, piece):
+    order = scatter_plan(number, dims)
+    left = tuple(sizes[dim] for dim in dims if dim not in order[: stage + 1])
+    return (sizes[order[stage]] - 1,) + left + piece[3:]
+
+
+def scatter_kernel(dims, sizes, pieces, count, *refs):
+    ins, outs = refs[:count], refs[count : 2 * count]
+    rest = list(refs[2 * count :])
+    depth = len(dims)
+    sums = rest[: len(pieces)]
+    landing = [
+        rest[len(pieces) + number * depth : len(pieces) + (number + 1) * depth]
+        for number in range(len(pieces))
+    ]
+    send_sem, recv_sem, load_sem = rest[-3:]
+    me = here(sizes)
+    greet(me, sizes, dims)
+    slot, _ = slots_of(dims, sizes)
+    held = [dim for dim in dims if dim != "core"]
+
+    def window(number, at):
+        item, row, column, high, wide = pieces[number]
+        index = tuple(at[dim] if dim == "core" else slice(None) for dim in dims)
+        return ins[item].at[index + (pl.ds(row, high), pl.ds(column, wide))]
+
+    loads = []
+    for number in range(len(pieces)):
+        load = pltpu.make_async_copy(window(number, me), sums[number], load_sem.at[number])
+        load.start()
+        loads.append(load)
+
+    sent = []
+
+    def copies(number, stage):
+        dim = scatter_plan(number, dims)[stage]
+        done = scatter_plan(number, dims)[:stage]
+        made = []
+        for step in range(1, sizes[dim]):
+            peer = moved(me, sizes, dim, step)
+            if dim == "core":
+                source = window(number, peer)
+            else:
+                index = tuple(
+                    peer[other] if other == dim else me[other] if other in done else slice(None)
+                    for other in held
+                )
+                source = sums[number].at[index]
+            place = slot[dim] + step - 1
+            made.append(
+                pltpu.make_async_remote_copy(
+                    src_ref=source,
+                    dst_ref=landing[number][stage].at[step - 1],
+                    send_sem=send_sem.at[number, place],
+                    recv_sem=recv_sem.at[number, place],
+                    device_id=device_of(peer, sizes),
+                    device_id_type=MESH,
+                )
+            )
+        return made
+
+    def reduce(number, stage):
+        item, row, column, high, wide = pieces[number]
+        order = scatter_plan(number, dims)
+        left = [dim for dim in held if dim not in order[: stage + 1]]
+        blocks = math.prod(sizes[dim] for dim in left)
+        tile = min(high, BLOCK_ROWS)
+        bands = high // tile
+
+        def body(turn, carry):
+            band = pl.ds(pl.multiple_of(lax.rem(turn, bands) * tile, tile), tile)
+            block = turn // bands
+            at = {}
+            for dim in reversed(left):
+                at[dim] = lax.rem(block, sizes[dim])
+                block = block // sizes[dim]
+            spot = tuple(at[dim] if dim in left else me[dim] for dim in held)
+            value = sums[number][spot + (band, slice(None))].astype(jnp.float32)
+            for step in range(1, sizes[order[stage]]):
+                arrived = landing[number][stage][
+                    (step - 1,) + tuple(at[dim] for dim in left) + (band, slice(None))
+                ]
+                value = value + arrived.astype(jnp.float32)
+            if stage == depth - 1:
+                start = pl.multiple_of(row + lax.rem(turn, bands) * tile, tile)
+                outs[item][pl.ds(start, tile), pl.ds(column, wide)] = value
+            else:
+                sums[number][spot + (band, slice(None))] = value.astype(jnp.bfloat16)
+            return carry
+
+        lax.fori_loop(0, blocks * bands, body, 0)
+
+    flights = {}
+    for tick in range(len(pieces) + depth):
+        for stage in range(depth, -1, -1):
+            number = tick - stage
+            if not 0 <= number < len(pieces):
+                continue
+            if stage > 0:
+                if stage == 1 and loads[number] is not None:
+                    loads[number].wait()
+                    loads[number] = None
+                for copy in flights[number, stage - 1]:
+                    copy.wait_recv()
+                reduce(number, stage - 1)
+            if stage < depth:
+                if stage == 0 and "core" not in dims:
+                    loads[number].wait()
+                    loads[number] = None
+                made = copies(number, stage)
+                for copy in made:
+                    copy.start()
+                    sent.append(copy)
+                flights[number, stage] = made
+    for copy in sent:
+        copy.wait_send()
+
+
+def scatter_blocks(blocks, dims, sizes, pieces, identity, limit):
+    count = len(blocks)
+    _, total = slots_of(dims, sizes)
+    held = tuple(sizes[dim] for dim in dims if dim != "core")
+    shapes = [b.shape[len(dims) :] for b in blocks]
+    scratch = [pltpu.VMEM(held + piece[3:], jnp.bfloat16) for piece in pieces]
+    for number, piece in enumerate(pieces):
+        for stage in range(len(dims)):
+            scratch.append(
+                pltpu.VMEM(landing_shape(number, stage, dims, sizes, piece), jnp.bfloat16)
+            )
+    return pl.pallas_call(
+        functools.partial(scatter_kernel, dims, sizes, pieces, count),
+        out_shape=[jax.ShapeDtypeStruct(shape, jnp.float32) for shape in shapes],
+        in_specs=[pl.BlockSpec(memory_space=pl.ANY)] * count,
+        out_specs=[pl.BlockSpec(memory_space=pltpu.VMEM)] * count,
+        scratch_shapes=scratch
+        + [
+            pltpu.SemaphoreType.DMA((len(pieces), total)),
+            pltpu.SemaphoreType.DMA((len(pieces), total)),
+            pltpu.SemaphoreType.DMA((len(pieces),)),
+        ],
+        compiler_params=pltpu.CompilerParams(
+            collective_id=identity, has_side_effects=True, vmem_limit_bytes=limit
+        ),
+    )(*blocks)
+
+
+ALL_DIMS = ("z", "core", "y", "x")
+SEQ_DIMS = ("y", "x")
+
+
+def tall(rows, columns):
+    if rows % 16 == 0:
+        return rows, columns
+    return 16, rows * columns // 16
+
+
+def gather_weights(matrices, vectors, sizes):
+    count = math.prod(sizes[dim] for dim in ALL_DIMS)
+    packed = jnp.concatenate(vectors)
+    packed = jnp.pad(packed, (0, 2048 - packed.size)).reshape(16, 128)
+    shards = [packed] + [m.reshape(tall(*m.shape)) for m in matrices]
+    pieces = pieces_of([s.shape for s in shards], BLOCK_ROWS, BLOCK_COLUMNS)
+    whole = gather_blocks(shards, ALL_DIMS, sizes, pieces, 0)
+    flat = whole[0].reshape(count, 2048)
+    parts, offset = [], 0
+    for vector in vectors:
+        parts.append(flat[:, offset : offset + vector.size].reshape(count * vector.size))
+        offset += vector.size
+    full = [
+        w.reshape(count * m.shape[0], m.shape[1]) for w, m in zip(whole[1:], matrices)
+    ]
+    return full, parts
+
+
+def scatter_grads(matrices, vectors, sizes):
+    count = math.prod(sizes[dim] for dim in ALL_DIMS)
+    front = tuple(sizes[dim] for dim in ALL_DIMS)
+    packed = jnp.concatenate([v.reshape(count, -1) for v in vectors], axis=1)
+    packed = jnp.pad(packed, ((0, 0), (0, 2048 - packed.shape[1]))).astype(jnp.bfloat16)
+    blocks = [packed.reshape(front + (16, 128))]
+    for matrix in matrices:
+        shape = tall(matrix.shape[0] // count, matrix.shape[1])
+        blocks.append(matrix.reshape(front + shape))
+    pieces = pieces_of([b.shape[4:] for b in blocks], BLOCK_ROWS, BLOCK_COLUMNS)
+    owned = scatter_blocks(blocks, ALL_DIMS, sizes, pieces, 1, 52 * 1024 * 1024)
+    flat = owned[0].reshape(2048)
+    parts, offset = [], 0
+    for vector in vectors:
+        part = vector.size // count
+        parts.append(flat[offset : offset + part])
+        offset += part
+    full = [
+        o.reshape(m.shape[0] // count, m.shape[1]) for o, m in zip(owned[1:], matrices)
+    ]
+    return full, parts
+
+
+def gather_sequence(arrays, sizes):
+    seqs, group, width = arrays[0].shape
+    count = sizes["x"] * sizes["y"]
+    shards = [a.reshape(seqs * group, width) for a in arrays]
+    pieces = pieces_of([s.shape for s in shards], seqs * group, 512)
+    whole = gather_blocks(shards, SEQ_DIMS, sizes, pieces, 2)
+    return [
+        jnp.moveaxis(w.reshape(count, seqs, group, width), 0, 1).reshape(
+            seqs, count * group, width
+        )
+        for w in whole
+    ]
+
+
+def scatter_sequence(arrays, sizes):
+    seqs, length, width = arrays[0].shape
+    count = sizes["x"] * sizes["y"]
+    group = length // count
+    front = (sizes["y"], sizes["x"])
+    blocks = [
+        jnp.moveaxis(a.reshape(seqs, count, group, width), 1, 0).reshape(
+            front + (seqs * group, width)
+        )
+        for a in arrays
+    ]
+    pieces = pieces_of([b.shape[2:] for b in blocks], seqs * group, 512)
+    owned = scatter_blocks(blocks, SEQ_DIMS, sizes, pieces, 3, 52 * 1024 * 1024)
+    return [o.reshape(seqs, group, width) for o in owned]
 
 
 def layer_norm(values, gain, shift):
@@ -65,20 +461,37 @@
     shrink_weight,
     shrink_bias,
 ):
+    sizes = lattice(lax.axis_size("fsdp"), lax.axis_size("seq"))
+    matrices, vectors = gather_weights(
+        (qkv_weight, output_weight, expand_weight, shrink_weight),
+        (
+            first_gain,
+            first_shift,
+            query_bias,
+            value_bias,
+            output_bias,
+            second_gain,
+            second_shift,
+            expand_bias,
+            shrink_bias,
+        ),
+        sizes,
+    )
+    qkv_full, output_full, expand_full, shrink_full = matrices
     forward_set = (
-        lax.all_gather(first_gain, ("fsdp", "seq"), axis=0, tiled=True),
-        lax.all_gather(first_shift, ("fsdp", "seq"), axis=0, tiled=True),
-        lax.all_gather(qkv_weight, ("fsdp", "seq"), axis=0, tiled=True),
-        lax.all_gather(query_bias, ("fsdp", "seq"), axis=0, tiled=True),
-        lax.all_gather(value_bias, ("fsdp", "seq"), axis=0, tiled=True),
-        lax.all_gather(output_weight, ("fsdp", "seq"), axis=0, tiled=True),
-        lax.all_gather(output_bias, ("fsdp", "seq"), axis=0, tiled=True),
-        lax.all_gather(second_gain, ("fsdp", "seq"), axis=0, tiled=True),
-        lax.all_gather(second_shift, ("fsdp", "seq"), axis=0, tiled=True),
-        lax.all_gather(expand_weight, ("fsdp", "seq"), axis=0, tiled=True),
-        lax.all_gather(expand_bias, ("fsdp", "seq"), axis=0, tiled=True),
-        lax.all_gather(shrink_weight, ("fsdp", "seq"), axis=0, tiled=True),
-        lax.all_gather(shrink_bias, ("fsdp", "seq"), axis=0, tiled=True),
+        vectors[0],
+        vectors[1],
+        qkv_full,
+        vectors[2],
+        vectors[3],
+        output_full,
+        vectors[4],
+        vectors[5],
+        vectors[6],
+        expand_full,
+        vectors[7],
+        shrink_full,
+        vectors[8],
     )
     seqs, group, width = inputs.shape
     length = segments.shape[1]
@@ -98,10 +511,7 @@
         .astype(jnp.bfloat16)
         .reshape(seqs, group, width)
     )
-    key_all, value_all = (
-        lax.all_gather(key_local, "seq", axis=1, tiled=True),
-        lax.all_gather(value_local, "seq", axis=1, tiled=True),
-    )
+    key_all, value_all = gather_sequence((key_local, value_local), sizes)
     first_place = lax.axis_index("seq") * group
     query_segment = lax.dynamic_slice_in_dim(segments, first_place, group, 1)
     query_place = first_place + jnp.arange(group)
@@ -129,21 +539,7 @@
         middle + rows_product(acts_third, forward_set[11]) + forward_set[12].astype(jnp.float32)
     )
     outputs = result.astype(jnp.bfloat16).reshape(seqs, group, width)
-    back_set = (
-        lax.all_gather(first_gain, ("fsdp", "seq"), axis=0, tiled=True),
-        lax.all_gather(first_shift, ("fsdp", "seq"), axis=0, tiled=True),
-        lax.all_gather(qkv_weight, ("fsdp", "seq"), axis=0, tiled=True),
-        lax.all_gather(query_bias, ("fsdp", "seq"), axis=0, tiled=True),
-        lax.all_gather(value_bias, ("fsdp", "seq"), axis=0, tiled=True),
-        lax.all_gather(output_weight, ("fsdp", "seq"), axis=0, tiled=True),
-        lax.all_gather(output_bias, ("fsdp", "seq"), axis=0, tiled=True),
-        lax.all_gather(second_gain, ("fsdp", "seq"), axis=0, tiled=True),
-        lax.all_gather(second_shift, ("fsdp", "seq"), axis=0, tiled=True),
-        lax.all_gather(expand_weight, ("fsdp", "seq"), axis=0, tiled=True),
-        lax.all_gather(expand_bias, ("fsdp", "seq"), axis=0, tiled=True),
-        lax.all_gather(shrink_weight, ("fsdp", "seq"), axis=0, tiled=True),
-        lax.all_gather(shrink_bias, ("fsdp", "seq"), axis=0, tiled=True),
-    )
+    back_set = forward_set
     grad_out = cotangent.reshape(rows, width)
     grad_shrink = weight_grad(acts_third, grad_out)
     grad_shrink_bias = column_sum(grad_out)
@@ -166,10 +562,7 @@
         .astype(jnp.bfloat16)
         .reshape(seqs, group, heads, HEAD_DIM)
     )
-    key_back, value_back = (
-        lax.all_gather(key_local, "seq", axis=1, tiled=True),
-        lax.all_gather(value_local, "seq", axis=1, tiled=True),
-    )
+    key_back, value_back = key_all, value_all
     key_heads = key_back.reshape(seqs, length, heads, HEAD_DIM)
     value_heads = value_back.reshape(seqs, length, heads, HEAD_DIM)
     scores_again = masked_scores(query_heads, key_heads, allowed)
@@ -193,19 +586,12 @@
         grad_mixed,
         preferred_element_type=jnp.float32,
     )
-    grad_key, grad_value = (
-        lax.psum_scatter(
+    grad_key, grad_value = scatter_sequence(
+        (
             key_terms.reshape(seqs, length, width).astype(jnp.bfloat16),
-            "seq",
-            scatter_dimension=1,
-            tiled=True,
-        ).astype(jnp.float32),
-        lax.psum_scatter(
             value_terms.reshape(seqs, length, width).astype(jnp.bfloat16),
-            "seq",
-            scatter_dimension=1,
-            tiled=True,
-        ).astype(jnp.float32),
+        ),
+        sizes,
     )
     grad_joined = jnp.concatenate(
         [
@@ -224,22 +610,41 @@
     )
     grad_tokens_norm, grad_gain_first, grad_shift_first = first_pull(grad_acts_first)
     grad_inputs = (grad_middle + grad_tokens_norm).astype(jnp.bfloat16).reshape(seqs, group, width)
-    owned = (
-        lax.psum_scatter(grad_gain_first, ("fsdp", "seq"), scatter_dimension=0, tiled=True),
-        lax.psum_scatter(grad_shift_first, ("fsdp", "seq"), scatter_dimension=0, tiled=True),
-        lax.psum_scatter(grad_qkv, ("fsdp", "seq"), scatter_dimension=0, tiled=True),
-        lax.psum_scatter(grad_query_bias, ("fsdp", "seq"), scatter_dimension=0, tiled=True),
-        lax.psum_scatter(grad_value_bias, ("fsdp", "seq"), scatter_dimension=0, tiled=True),
-        lax.psum_scatter(grad_output, ("fsdp", "seq"), scatter_dimension=0, tiled=True),
-        lax.psum_scatter(grad_output_bias, ("fsdp", "seq"), scatter_dimension=0, tiled=True),
-        lax.psum_scatter(grad_gain_second, ("fsdp", "seq"), scatter_dimension=0, tiled=True),
-        lax.psum_scatter(grad_shift_second, ("fsdp", "seq"), scatter_dimension=0, tiled=True),
-        lax.psum_scatter(grad_expand, ("fsdp", "seq"), scatter_dimension=0, tiled=True),
-        lax.psum_scatter(grad_expand_bias, ("fsdp", "seq"), scatter_dimension=0, tiled=True),
-        lax.psum_scatter(grad_shrink, ("fsdp", "seq"), scatter_dimension=0, tiled=True),
-        lax.psum_scatter(grad_shrink_bias, ("fsdp", "seq"), scatter_dimension=0, tiled=True),
-    )
-    return (outputs, grad_inputs) + tuple(owned)
+    owned, parts = scatter_grads(
+        tuple(
+            grad.astype(jnp.bfloat16)
+            for grad in (grad_qkv, grad_output, grad_expand, grad_shrink)
+        ),
+        (
+            grad_gain_first,
+            grad_shift_first,
+            grad_query_bias,
+            grad_value_bias,
+            grad_output_bias,
+            grad_gain_second,
+            grad_shift_second,
+            grad_expand_bias,
+            grad_shrink_bias,
+        ),
+        sizes,
+    )
+    return (
+        outputs,
+        grad_inputs,
+        parts[0],
+        parts[1],
+        owned[0],
+        parts[2],
+        parts[3],
+        owned[1],
+        parts[4],
+        parts[5],
+        parts[6],
+        owned[2],
+        parts[7],
+        owned[3],
+        parts[8],
+    )
 
 
 def solution(mesh):

time: 1520 us -> 743 us (0.49)
  waiting for transfers between devices: 1170 us -> 0 us
  Pallas kernels: 0 us -> 548 us
  blocking collectives: 149 us -> 0 us
  local copies, waits for them, and re-layouts: 25.7 us -> 61.9 us
  matrix products: 125 us -> 104 us
    reduce_scatter x6 -> x0, waiting for transfers between devices: 966 us -> none  [the longest x1 362 us: local(): lax.psum_scatter(grad_expand, ('fsdp', 'seq'), scatter_dimension=0, tiled...]
    pallas_call x0 -> x4, Pallas kernels: none -> 548 us  [the longest x2 286 us: scatter_blocks(): pl.pallas_call(functools.partial(scatter_kernel, dims, sizes, pieces, cou...]
    all_gather x6 -> x0, waiting for transfers between devices: 206 us -> none  [the longest x1 76.5 us: local(): lax.all_gather(expand_weight, ('fsdp', 'seq'), axis=0, tiled=True)]
    unnamed x2 -> x0, blocking collectives: 83.8 us -> none
    all_gather x1 -> x0, blocking collectives: 65.7 us -> none  [local(): lax.all_gather(expand_bias, ('fsdp', 'seq'), axis=0, tiled=True)]
    convert_element_type x0 -> x12, local copies, waits for them, and re-layouts: none -> 22.6 us  [the longest x2 10.7 us: local(): key_terms.reshape(seqs, length, width).astype(jnp.bfloat16)]
  transfers between devices with their start and end apart: 12 -> 0, of which waited for: 9 -> 0; matrix products, arithmetic and copies ran while one was open for 9% -> 0% of each run, Pallas kernels for 0% -> 0%
where the time goes in v1:
time: 743 us; the launch traced here: 738 us
  Pallas kernels  548 us (74%)
  matrix products  104 us (14%)
  local copies, waits for them, and re-layouts  61.9 us (8%)
  other arithmetic  22.2 us (3%)
    pallas_call x2, Pallas kernels, scatter_blocks(): pl.pallas_call(functools.partial(scatter_kernel, dims, sizes, pieces, cou...  286 us
    pallas_call x2, Pallas kernels, gather_blocks(): pl.pallas_call(functools.partial(gather_kernel, dims, sizes, pieces, coun...  262 us
    dot_general x4, matrix products, rows_product(): return jnp.dot(left, right, preferred_element_type=jnp.float32)  20.2 us
    dot_general x4, matrix products, weight_grad(): lax.dot_general(left, right, (((0,), (0,)), ((), ())), preferred_element_...  19.4 us
    dot_general x4, matrix products, input_grad(): lax.dot_general(left, right, (((1,), (1,)), ((), ())), preferred_element_...  15.5 us

profile of v1, /device:TPU:0, one launch (start us, length us, event | category | flops | bytes accessed | tf_op | source)
XLA Modules:
  0.0 737.9 jit_solution(15046966785741399833)
XLA Ops:
  0.6 6.1 concatenate.11
  7.3 175.7 %shard_map.274 = (bf16[4,2,2,2,16,128]{5,4,3,2,1,0:T(8,128)(2,1)}, bf16[4,2,2,2,32,3072]{5,4,3,2,1,0:T(8,128)(2,1)}, bf16[4,2,2,2,32,1024]{5,4,3,2,1,0:T(8,128)(...) custom-call(bf16[16,128]{1,0:T(8,128)(2,1)} %pad_bitcast_fusion.1.refs_0_, ...), custom_call_target="tpu_custom_call" | custom-call | tf_op jit(solution)/shard_map/pallas_call | solution.py:159
  188.1 4.9 fusion.51
  195.3 86.6 %shard_map.275 = (bf16[2,2,256,1024]{3,2,1,0:T(8,128)(2,1)}, bf16[2,2,256,1024]{3,2,1,0:T(8,128)(2,1)}) custom-call(bf16[256,1024]{1,0:T(8,128)(2,1)} %slice.129.refs_0_, bf16[256,1024]{1,0:T(8,128)(2,1)} %get-tuple-element.57.refs_1_), custom_call_target="tpu_custom_call" | custom-call | tf_op jit(solution)/shard_map/pallas_call | solution.py:159
  281.9 5.0 copy.42
  287.0 2.7 reshape.445
  290.2 6.4 copy.44
  296.6 3.2 reshape.447
  299.9 9.4 %fusion.78 = (f32[16,256]{1,0:T(8,128)S(1)}, f32[16,256,1024]{2,1,0:T(8,128)}) fusion(pred[256,1024]{1,0:T(8,128)(4,1)S(1)} %fusion.46, bf16[256,16,64]{0,2,1:T(8,128)(2,1)S(1)} %bitcast.150, bf16[1024,16,64]{0,2,1:T(8,128)(2,1)S(1)} %reshape.447), kind=kOutput, calls=%fused_computation.131 | convolution fusion | flops 553649152 | bytes 19677184 | tf_op jit(solution)/shard_map/sub | solution.py:524
  309.3 9.3 %fusion.29 = bf16[16,64,256]{2,1,0:T(8,128)(2,1)S(1)} fusion(bf16[1024,16,64]{0,2,1:T(8,128)(2,1)} %reshape.445, f32[16,256,1024]{2,1,0:T(8,128)} %get-tuple-element.75, f32[16,256]{1,0:T(8,128)S(1)} %get-tuple-element.74), kind=kOutput, calls=%fused_computation.54 | convolution fusion | flops 545521664 | bytes 19415040 | tf_op jit(solution)/shard_map/bhqk,bkhd->bqhd/dot_general | solution.py:527
  320.1 6.0 convolution_add_fusion
  326.1 8.5 %fusion.32 = bf16[1,256,1024]{2,1,0:T(8,128)(2,1)} fusion(f32[256,1024]{1,0:T(8,128)S(1)} %get-tuple-element.77, bf16[4096,1024]{1,0:T(8,128)(2,1)} %bitcast.169, f32[1024]{0:T(1024)S(1)} %reshape.480, f32[256,4096]{1,0:T(8,128)S(1)} %convolution_add_fusion), kind=kOutput, calls=%fused_computation.55 | convolution fusion | flops 2157707264 | bytes 14159872 | tf_op jit(solution)/shard_map/dot_general | solution.py:420
  334.6 6.0 fusion.80
  340.7 2.7 multiply_reduce_fusion.1
  348.5 11.4 %multiply_reduce_fusion = (f32[16,256]{1,0:T(8,128)S(1)}, f32[16,256,1024]{2,1,0:T(8,128)}) fusion(f32[16,256,1024]{2,1,0:T(8,128)} %get-tuple-element.75, f32[16,256]{1,0:T(8,128)S(1)} %copy-done.22, bf16[256,16,64]{0,2,1:T(8,128)(2,1)} %bitcast.157, bf16[1024,16,64]{0,2,1:T(8,128)(2,1)} %reshape.445), kind=kOutput, calls=%fused_computation.2 | convolution fusion | flops 549449728 | bytes 36208640 | tf_op jit(solution)/shard_map/bqhd,bkhd->bhqk/dot_general | solution.py:570
  359.9 11.6 %multiply_convert_fusion = bf16[16,256,1024]{2,1,0:T(8,128)(2,1)S(1)} fusion(f32[16,256,1024]{2,1,0:T(8,128)} %get-tuple-element.80, f32[16,256]{1,0:T(8,128)S(1)} %get-tuple-element.79, f32[16,256,1024]{2,1,0:T(8,128)} %get-tuple-element.75, f32[16,256]{1,0:T(8,128)S(1)} %copy-done.22), kind=kLoop, calls=%fused_computation.1 | loop fusion | flops 16777216 | bytes 41975808 | tf_op jit(solution)/shard_map/convert_element_type | solution.py:574
  371.5 3.2 copy-done
  374.7 3.0 fusion.19
  377.7 4.5 convert_element_type.263
  382.2 6.2 copy.46.refs_0_
  388.4 9.2 %convert_bitcast_fusion = bf16[1,1024,16,64]{1,3,2,0:T(8,128)(2,1)} fusion(bf16[256,16,64]{0,2,1:T(8,128)(2,1)} %bitcast.158, f32[16,256,1024]{2,1,0:T(8,128)} %get-tuple-element.75, f32[16,256]{1,0:T(8,128)S(1)} %copy-done.22), kind=kOutput, calls=%fused_computation.31 | convolution fusion | flops 546308096 | bytes 19415040 | tf_op jit(solution)/shard_map/bhqk,bqhd->bkhd/dot_general | solution.py:583
  397.6 4.5 convert_element_type.267
  402.1 6.2 copy.47.refs_1_
  408.3 66.4 %shard_map.276 = (f32[256,1024]{1,0:T(8,128)S(1)}, f32[256,1024]{1,0:T(8,128)}) custom-call(bf16[2,2,256,1024]{3,2,1,0:T(8,128)(2,1)} %copy.46.refs_0_, bf16[2,2,256,1024]{3,2,1,0:T(8,128)(2,1)} %copy.47.refs_1_), custom_call_target="tpu_custom_call" | custom-call | tf_op jit(solution)/shard_map/pallas_call | solution.py:307
  474.7 2.1 fusion.75
  477.6 6.8 bitcast_reduce_fusion
  484.5 2.1 copy.48
  486.6 5.3 fusion.72
  494.7 6.1 convolution_convert_fusion.2
  502.9 5.7 convolution_convert_fusion.1
  508.6 5.4 convolution_convert_fusion
  514.0 219.5 %shard_map.277 = (f32[16,128]{1,0:T(8,128)S(1)}, f32[32,3072]{1,0:T(8,128)S(1)}, f32[32,1024]{1,0:T(8,128)S(1)}, f32[32,4096]{1,0:T(8,128)S(1)}, f32[128,1024]{1,0:T(8,128)S(1)}) custom-call(bf16[4,2,2,2,16,128]{5,4,3,2,1,0:T(8,128)(2,1)S(1)} %bitcast.143, bf16[4,2,2,2,32,3072]{5,4,3,2,1,0:T(8,128)(2,1)} %bitcast.149, ...), custom_call_target="tpu_custom_call" | custom-call | tf_op jit(solution)/shard_map/pallas_call | solution.py:307
  (133 shorter events, 24.8 us)
Async XLA Ops:
  185.5 7.5 %copy-start.30 = (f32[1024]{0:T(1024)}, f32[1024]{0:T(1024)S(1)}, u32[]{:S(2)}) copy-start(f32[1024]{0:T(1024)S(1)} %reshape.473) | copy-start | bytes 12292
  185.5 7.5 %copy-start.19 = (f32[1024]{0:T(1024)}, f32[1024]{0:T(1024)S(1)}, u32[]{:S(2)}) copy-start(f32[1024]{0:T(1024)S(1)} %reshape.472) | copy-start | bytes 12292
  186.7 6.3 copy-start.23
  188.1 4.9 copy-start.25
  188.1 4.9 copy-start.27
  281.9 7.8 %copy-start.29 = (s32[1,1024]{1,0:T(1,128)S(1)}, s32[1,1024]{1,0:T(1,128)}, u32[]{:S(2)}) copy-start(s32[1,1024]{1,0:T(1,128)} %param.17) | copy-start | bytes 12292
  281.9 8.1 %copy-start.15 = (bf16[256,1024]{1,0:T(8,128)(2,1)S(1)}, bf16[256,1024]{1,0:T(8,128)(2,1)}, u32[]{:S(2)}) copy-start(bf16[256,1024]{1,0:T(8,128)(2,1)} %get-tuple-element.56) | copy-start | bytes 1572868
  290.2 9.6 %copy-start.5 = (bf16[256,1024]{0,1:T(8,128)(2,1)}, bf16[256,1024]{0,1:T(8,128)(2,1)S(1)}, u32[]{:S(2)}) copy-start(bf16[256,1024]{0,1:T(8,128)(2,1)S(1)} %copy.43) | copy-start | bytes 1572868
  299.8 9.4 %copy-start.2 = (bf16[1024,16,64]{0,2,1:T(8,128)(2,1)}, bf16[1024,16,64]{0,2,1:T(8,128)(2,1)S(1)}, u32[]{:S(2)}) copy-start(bf16[1024,16,64]{0,2,1:T(8,128)(2,1)S(1)} %reshape.447) | copy-start | bytes 6291460
  309.3 9.3 %copy-start.21 = (f32[16,256]{1,0:T(8,128)}, f32[16,256]{1,0:T(8,128)S(1)}, u32[]{:S(2)}) copy-start(f32[16,256]{1,0:T(8,128)S(1)} %get-tuple-element.74) | copy-start | bytes 49156
  309.3 9.3 %copy-start.1 = (bf16[1,256,1024]{2,1,0:T(8,128)(2,1)S(1)}, bf16[1,256,1024]{2,1,0:T(8,128)(2,1)}, u32[]{:S(2)}) copy-start(bf16[1,256,1024]{2,1,0:T(8,128)(2,1)} %param.16) | copy-start | bytes 1572868
  309.3 9.4 %copy-start.9 = (bf16[4,2,2,2,32,1024]{5,4,3,2,1,0:T(8,128)(2,1)S(1)}, bf16[4,2,2,2,32,1024]{5,4,3,2,1,0:T(8,128)(2,1)}, u32[]{:S(2)}) copy-start(bf16[4,2,2,2,32,1024]{5,4,3,2,1,0:T(8,128)(2,1)} %get-tuple-element.33) | copy-start | bytes 6291460
  309.3 9.4 %copy-start.18 = (f32[1024]{0:T(1024)S(1)}, f32[1024]{0:T(1024)}, u32[]{:S(2)}) copy-start(f32[1024]{0:T(1024)} %reshape.476) | copy-start | bytes 12292
  320.1 14.5 %slice-start.2 = ((s8[8388608]{0:T(1024)(128)(4,1)}), s8[4194304]{0:T(1024)(128)(4,1)S(1)}, s32[]{:S(2)}) async-start(s8[8388608]{0:T(1024)(128)(4,1)} %bitcast.170), calls=%async_computation.2 | async-start | bytes 8388608
  326.0 8.5 %copy-start.32 = (f32[256,4096]{1,0:T(8,128)}, f32[256,4096]{1,0:T(8,128)S(1)}, u32[]{:S(2)}) copy-start(f32[256,4096]{1,0:T(8,128)S(1)} %convolution_add_fusion) | copy-start | bytes 12582916
  326.1 8.5 %copy-start.4 = (bf16[1,256,1024]{2,1,0:T(8,128)(2,1)S(1)}, bf16[1,256,1024]{2,1,0:T(8,128)(2,1)}, u32[]{:S(2)}) copy-start(bf16[1,256,1024]{2,1,0:T(8,128)(2,1)} %param.18) | copy-start | bytes 1572868
  326.1 8.5 %slice-start.3 = ((s8[8388608]{0:T(1024)(128)(4,1)}), s8[4194304]{0:T(1024)(128)(4,1)S(1)}, s32[]{:S(2)}) async-start(s8[8388608]{0:T(1024)(128)(4,1)} %bitcast.170), calls=%async_computation.3 | async-start | bytes 8388608
  326.1 14.6 %slice-start = ((s8[8388608]{0:T(1024)(128)(4,1)}), s8[4194304]{0:T(1024)(128)(4,1)S(1)}, s32[]{:S(2)}) async-start(s8[8388608]{0:T(1024)(128)(4,1)} %bitcast.166), calls=%async_computation | async-start | bytes 8388608
  334.6 6.1 slice-start.1
  343.4 5.1 copy-start.22
  359.9 14.8 %copy-start.6 = (bf16[256,1024]{0,1:T(8,128)(2,1)S(1)}, bf16[256,1024]{0,1:T(8,128)(2,1)}, u32[]{:S(2)}) copy-start(bf16[256,1024]{0,1:T(8,128)(2,1)} %copy-done.5) | copy-start | bytes 1572868
  371.5 3.2 copy-start
  408.3 69.3 %copy-start.3 = (bf16[1024,16,64]{0,2,1:T(8,128)(2,1)S(1)}, bf16[1024,16,64]{0,2,1:T(8,128)(2,1)}, u32[]{:S(2)}) copy-start(bf16[1024,16,64]{0,2,1:T(8,128)(2,1)} %copy-done.2) | copy-start | bytes 6291460
  477.6 8.9 %copy-start.20 = (f32[1024]{0:T(1024)S(1)}, f32[1024]{0:T(1024)}, u32[]{:S(2)}) copy-start(f32[1024]{0:T(1024)} %copy-done.19) | copy-start | bytes 12292
  477.6 8.9 %copy-start.24 = (f32[256]{0:T(256)S(1)}, f32[256]{0:T(256)}, u32[]{:S(2)}) copy-start(f32[256]{0:T(256)} %copy-done.23) | copy-start | bytes 3076
  486.6 5.3 copy-start.26
  486.6 5.3 copy-start.28
  491.8 2.8 copy-start.31
  494.6 6.2 copy-start.12
  494.7 6.2 copy-start.14
  494.7 8.2 %copy-start.8 = (bf16[256,4096]{1,0:T(8,128)(2,1)S(1)}, bf16[256,4096]{1,0:T(8,128)(2,1)}, u32[]{:S(2)}) copy-start(bf16[256,4096]{1,0:T(8,128)(2,1)} %copy-done.7) | copy-start | bytes 6291460
  502.9 5.7 copy-start.33
  (6 other events, 7.9 us)

commit v2 on v1

--- a/solution.py
+++ b/solution.py
@@ -12,6 +12,7 @@
 
 BLOCK_ROWS = 32
 BLOCK_COLUMNS = 1024
+LAG = 2
 MESH = pl.DeviceIdType.MESH
 
 
@@ -92,8 +93,9 @@
     own_waited = set()
 
     def order_of(number):
-        across = ("x", "y") if number % 2 == 0 else ("y", "x")
-        return [dim for dim in ("z",) + across + ("core",) if dim in dims]
+        one, two = ("x", "y") if number % 2 == 0 else ("y", "x")
+        order = (one, "z", two) if number % 3 == 1 else ("z", one, two)
+        return [dim for dim in order + ("core",) if dim in dims]
 
     def region(number, stage, at):
         item, row, column, high, wide = pieces[number]
@@ -121,9 +123,9 @@
 
     sent = []
     depth = len(dims)
-    for tick in range(len(pieces) + depth):
-        for stage in range(depth, -1, -1):
-            number = tick - stage
+    for tick in range(len(pieces) + LAG * depth):
+        for stage in range(depth + 1):
+            number = tick - LAG * stage
             if not 0 <= number < len(pieces):
                 continue
             item, row, column, high, wide = pieces[number]
@@ -159,7 +161,7 @@
     return pl.pallas_call(
         functools.partial(gather_kernel, dims, sizes, pieces, count),
         out_shape=[jax.ShapeDtypeStruct(front + s.shape, s.dtype) for s in shards],
-        in_specs=[pl.BlockSpec(memory_space=pl.ANY)] * count,
+        in_specs=[pl.BlockSpec(memory_space=pltpu.VMEM)] * count,
         out_specs=[pl.BlockSpec(memory_space=pl.ANY)] * count,
         scratch_shapes=[
             pltpu.SemaphoreType.DMA((len(pieces), total)),
@@ -171,8 +173,9 @@
 
 
 def scatter_plan(number, dims):
-    across = ("x", "y") if number % 2 == 0 else ("y", "x")
-    return [dim for dim in ("core",) + across + ("z",) if dim in dims]
+    one, two = ("x", "y") if number % 2 == 0 else ("y", "x")
+    order = (one, "z", two) if number % 3 == 2 else (one, two, "z")
+    return [dim for dim in ("core",) + order if dim in dims]
 
 
 def landing_shape(number, stage, dims, sizes, piece):
@@ -268,27 +271,30 @@
         lax.fori_loop(0, blocks * bands, body, 0)
 
     flights = {}
-    for tick in range(len(pieces) + depth):
-        for stage in range(depth, -1, -1):
-            number = tick - stage
+
+    def launch(number, stage):
+        flights[number, stage] = copies(number, stage)
+        for copy in flights[number, stage]:
+            copy.start()
+            sent.append(copy)
+
+    if "core" in dims:
+        for number in range(len(pieces)):
+            launch(number, 0)
+    first = 1 if "core" in dims else 0
+    for tick in range(len(pieces) + LAG * depth):
+        for stage in range(first, depth + 1):
+            number = tick - LAG * (stage - first)
             if not 0 <= number < len(pieces):
                 continue
+            if stage == first:
+                loads[number].wait()
             if stage > 0:
-                if stage == 1 and loads[number] is not None:
-                    loads[number].wait()
-                    loads[number] = None
                 for copy in flights[number, stage - 1]:
                     copy.wait_recv()
                 reduce(number, stage - 1)
             if stage < depth:
-                if stage == 0 and "core" not in dims:
-                    loads[number].wait()
-                    loads[number] = None
-                made = copies(number, stage)
-                for copy in made:
-                    copy.start()
-                    sent.append(copy)
-                flights[number, stage] = made
+                launch(number, stage)
     for copy in sent:
         copy.wait_send()
 
@@ -436,11 +442,77 @@
     return jnp.sum(values.astype(jnp.float32), axis=0)
 
 
-def masked_scores(queries, keys, allowed):
-    scores = (
-        jnp.einsum("bqhd,bkhd->bhqk", queries, keys, preferred_element_type=jnp.float32) * 0.125
-    )
-    return jnp.where(allowed, scores, -1e30)
+def attend_kernel(query, key, value, mask, mixed):
+    lane = lax.broadcasted_iota(jnp.int32, (1, query.shape[-1]), 1)
+    total = jnp.zeros(query.shape[1:], jnp.float32)
+    for head in range(query.shape[-1] // HEAD_DIM):
+        own = (lane // HEAD_DIM == head).astype(jnp.bfloat16)
+        scores = input_grad(query[0] * (own * 0.125), key[0])
+        scores = jnp.where(mask[0] > 0, scores, -1e30)
+        largest = jnp.max(scores, axis=-1, keepdims=True)
+        expon = jnp.exp(scores - largest)
+        scale = 1.0 / jnp.sum(expon, axis=-1, keepdims=True)
+        probs = (expon * scale).astype(jnp.bfloat16)
+        total = total + rows_product(probs, value[0] * own)
+    mixed[0] = total.astype(jnp.bfloat16)
+
+
+def attend_back_kernel(query, key, value, grad, mask, grad_query, grad_key, grad_value):
+    lane = lax.broadcasted_iota(jnp.int32, (1, query.shape[-1]), 1)
+    query_total = jnp.zeros(query.shape[1:], jnp.float32)
+    key_total = jnp.zeros(key.shape[1:], jnp.float32)
+    value_total = jnp.zeros(value.shape[1:], jnp.float32)
+    for head in range(query.shape[-1] // HEAD_DIM):
+        own = (lane // HEAD_DIM == head).astype(jnp.bfloat16)
+        head_query = query[0] * (own * 0.125)
+        head_grad = grad[0] * own
+        scores = input_grad(key[0], head_query)
+        scores = jnp.where(mask[0] > 0, scores, -1e30)
+        largest = jnp.max(scores, axis=0, keepdims=True)
+        expon = jnp.exp(scores - largest)
+        probs = expon * (1.0 / jnp.sum(expon, axis=0, keepdims=True))
+        grad_probs = input_grad(value[0], head_grad)
+        centred = jnp.sum(probs * grad_probs, axis=0, keepdims=True)
+        grad_scores = (probs * (grad_probs - centred)).astype(jnp.bfloat16)
+        query_total = query_total + weight_grad(grad_scores, key[0] * own)
+        key_total = key_total + rows_product(grad_scores, head_query)
+        value_total = value_total + rows_product(probs.astype(jnp.bfloat16), head_grad)
+    grad_query[0] = (query_total * 0.125).astype(jnp.bfloat16)
+    grad_key[0] = key_total.astype(jnp.bfloat16)
+    grad_value[0] = value_total.astype(jnp.bfloat16)
+
+
+def pair_specs(lengths, mask_shape):
+    specs = [pl.BlockSpec((1, length, 128), lambda b, h: (b, 0, h)) for length in lengths]
+    return specs, pl.BlockSpec((1,) + mask_shape, lambda b, h: (b, 0, 0))
+
+
+def attend(query, key, value, mask):
+    seqs, group, width = query.shape
+    length = key.shape[1]
+    specs, mask_spec = pair_specs((group, length, length), (group, length))
+    return pl.pallas_call(
+        attend_kernel,
+        grid=(seqs, width // 128),
+        out_shape=jax.ShapeDtypeStruct(query.shape, jnp.bfloat16),
+        in_specs=specs + [mask_spec],
+        out_specs=specs[0],
+        compiler_params=pltpu.CompilerParams(vmem_limit_bytes=40 * 1024 * 1024),
+    )(query, key, value, mask)
+
+
+def attend_back(query, key, value, grad, mask):
+    seqs, group, width = query.shape
+    length = key.shape[1]
+    specs, mask_spec = pair_specs((group, length, length, group), (length, group))
+    return pl.pallas_call(
+        attend_back_kernel,
+        grid=(seqs, width // 128),
+        out_shape=[jax.ShapeDtypeStruct(a.shape, jnp.bfloat16) for a in (query, key, value)],
+        in_specs=specs + [mask_spec],
+        out_specs=specs[:3],
+        compiler_params=pltpu.CompilerParams(vmem_limit_bytes=48 * 1024 * 1024),
+    )(query, key, value, grad, mask)
 
 
 def local(
@@ -495,7 +567,6 @@
     )
     seqs, group, width = inputs.shape
     length = segments.shape[1]
-    heads = width // HEAD_DIM
     rows = seqs * group
     gain_first = forward_set[0].astype(jnp.float32)
     shift_first = forward_set[1].astype(jnp.float32)
@@ -517,20 +588,10 @@
     query_place = first_place + jnp.arange(group)
     key_place = jnp.arange(length)
     causal = key_place[None, :] <= query_place[:, None]
-    allowed = (causal[None] & (query_segment[:, :, None] == segments[:, None, :]))[:, None]
-    query_heads = query_rows.reshape(seqs, group, heads, HEAD_DIM)
-    scores = masked_scores(query_heads, key_all.reshape(seqs, length, heads, HEAD_DIM), allowed)
-    largest = jnp.max(scores, axis=-1, keepdims=True)
-    expon = jnp.exp(scores - largest)
-    total = jnp.sum(expon, axis=-1, keepdims=True)
-    probs = (expon / total).astype(jnp.bfloat16)
-    mixed = jnp.einsum(
-        "bhqk,bkhd->bqhd",
-        probs,
-        value_all.reshape(seqs, length, heads, HEAD_DIM),
-        preferred_element_type=jnp.float32,
-    )
-    mixed = mixed.reshape(rows, width).astype(jnp.bfloat16)
+    allowed = causal[None] & (query_segment[:, :, None] == segments[:, None, :])
+    allowed = allowed.astype(jnp.float32)
+    queries = query_rows.reshape(seqs, group, width)
+    mixed = attend(queries, key_all, value_all, allowed).reshape(rows, width)
     middle = tokens + rows_product(mixed, forward_set[5]) + forward_set[6].astype(jnp.float32)
     acts_second = layer_norm(middle, gain_second, shift_second).astype(jnp.bfloat16)
     hidden_pre = rows_product(acts_second, forward_set[9]) + forward_set[10].astype(jnp.float32)
@@ -558,49 +619,23 @@
     grad_output = weight_grad(mixed, grad_branch)
     grad_output_bias = column_sum(grad_branch)
     grad_mixed = (
-        input_grad(grad_branch, back_set[5])
-        .astype(jnp.bfloat16)
-        .reshape(seqs, group, heads, HEAD_DIM)
-    )
-    key_back, value_back = key_all, value_all
-    key_heads = key_back.reshape(seqs, length, heads, HEAD_DIM)
-    value_heads = value_back.reshape(seqs, length, heads, HEAD_DIM)
-    scores_again = masked_scores(query_heads, key_heads, allowed)
-    probs_again = jnp.exp(scores_again - largest) / total
-    grad_probs = jnp.einsum(
-        "bqhd,bkhd->bhqk", grad_mixed, value_heads, preferred_element_type=jnp.float32
-    )
-    centred = jnp.sum(probs_again * grad_probs, axis=-1, keepdims=True)
-    grad_scores = (probs_again * (grad_probs - centred)).astype(jnp.bfloat16)
-    grad_query = (
-        jnp.einsum("bhqk,bkhd->bqhd", grad_scores, key_heads, preferred_element_type=jnp.float32)
-        * 0.125
-    )
-    key_terms = (
-        jnp.einsum("bhqk,bqhd->bkhd", grad_scores, query_heads, preferred_element_type=jnp.float32)
-        * 0.125
-    )
-    value_terms = jnp.einsum(
-        "bhqk,bqhd->bkhd",
-        probs_again.astype(jnp.bfloat16),
-        grad_mixed,
-        preferred_element_type=jnp.float32,
+        input_grad(grad_branch, back_set[5]).astype(jnp.bfloat16).reshape(seqs, group, width)
+    )
+    grad_query, key_terms, value_terms = attend_back(
+        queries, key_all, value_all, grad_mixed, allowed.swapaxes(1, 2)
     )
     grad_key, grad_value = scatter_sequence(
-        (
-            key_terms.reshape(seqs, length, width).astype(jnp.bfloat16),
-            value_terms.reshape(seqs, length, width).astype(jnp.bfloat16),
-        ),
+        (key_terms, value_terms),
         sizes,
     )
     grad_joined = jnp.concatenate(
         [
             grad_query.reshape(rows, width),
-            grad_key.reshape(rows, width),
-            grad_value.reshape(rows, width),
+            grad_key.reshape(rows, width).astype(jnp.bfloat16),
+            grad_value.reshape(rows, width).astype(jnp.bfloat16),
         ],
         axis=1,
-    ).astype(jnp.bfloat16)
+    )
     grad_qkv = weight_grad(acts_first, grad_joined)
     grad_query_bias = column_sum(grad_joined[:, :width])
     grad_value_bias = column_sum(grad_joined[:, 2 * width :])

time: 743 us -> 451 us (0.61)
  Pallas kernels: 548 us -> 362 us
  matrix products: 104 us -> 50.5 us
  local copies, waits for them, and re-layouts: 61.9 us -> 23 us
  other arithmetic: 22.2 us -> 12.2 us
    pallas_call x2, Pallas kernels: 286 us -> 161 us  [scatter_blocks(): pl.pallas_call(functools.partial(scatter_kernel, dims, sizes, pieces, cou...]
    pallas_call x2, Pallas kernels: 262 us -> 166 us  [gather_blocks(): pl.pallas_call(functools.partial(gather_kernel, dims, sizes, pieces, coun...]
    dot_general x5 -> x0, matrix products: 39.7 us -> none  [the longest x1 11.4 us: local(): jnp.einsum('bqhd,bkhd->bhqk', grad_mixed, value_heads, preferred_element_...]
    pallas_call x0 -> x2, Pallas kernels: none -> 35.5 us  [the longest x1 22.7 us: attend_back(): pl.pallas_call(attend_back_kernel, grid=(seqs, width // 128), out_shape=[...]
    convert_element_type x6 -> x1, local copies, waits for them, and re-layouts: 23.6 us -> 2.54 us  [local(): allowed = allowed.astype(jnp.float32)]
    pallas_call x2 -> x0, local copies, waits for them, and re-layouts: 11.4 us -> none  [gather_blocks(): pl.pallas_call(functools.partial(gather_kernel, dims, sizes, pieces, coun...]
    sub x1 -> x0, matrix products: 9.41 us -> none  [local(): expon = jnp.exp(scores - largest)]
    convert_element_type x2, other arithmetic: 12.8 us -> 3.55 us  [the longest x1 2.6 us: local(): value_local = (joined[:, 2 * width:] + forward_set[4].astype(jnp.float32)...]
where the time goes in v2:
time: 451 us; the launch traced here: 448 us
  Pallas kernels  362 us (80%)
  matrix products  50.5 us (11%)
  local copies, waits for them, and re-layouts  23 us (5%)
  other arithmetic  12.2 us (3%)
    pallas_call x2, Pallas kernels, gather_blocks(): pl.pallas_call(functools.partial(gather_kernel, dims, sizes, pieces, coun...  166 us
    pallas_call x2, Pallas kernels, scatter_blocks(): pl.pallas_call(functools.partial(scatter_kernel, dims, sizes, pieces, cou...  161 us
    pallas_call x1, Pallas kernels, attend_back(): pl.pallas_call(attend_back_kernel, grid=(seqs, width // 128), out_shape=[...  22.7 us
    dot_general x4, matrix products, weight_grad(): lax.dot_general(left, right, (((0,), (0,)), ((), ())), preferred_element_...  19.1 us
    dot_general x4, matrix products, rows_product(): return jnp.dot(left, right, preferred_element_type=jnp.float32)  17 us
    dot_general x4, matrix products, input_grad(): lax.dot_general(left, right, (((1,), (1,)), ((), ())), preferred_element_...  14.4 us
    pallas_call x1, Pallas kernels, attend(): pl.pallas_call(attend_kernel, grid=(seqs, width // 128), out_shape=jax.Sh...  12.8 us
    unnamed x53, local copies, waits for them, and re-layouts  9.13 us

profile of v2, /device:TPU:0, one launch (start us, length us, event | category | flops | bytes accessed | tf_op | source)
XLA Modules:
  0.0 448.3 jit_solution(10053166696158564087)
XLA Ops:
  0.6 6.1 %concatenate.10 = bf16[384]{0:T(512)(128)(2,1)S(1)} concatenate(bf16[32]{0:T(256)(128)(2,1)} %param.19, bf16[32]{0:T(256)(128)(2,1)} %param.20, bf16[32]{0:T(256)(128)(2,1)} %param.22, bf16[32]{0:T(256)(128)(2,1)} %param.23, bf16[32]{0:T(256)(128)(2,1)} %param.25, bf16[32]{0:T(256)(128)(2,1)} %param.26, bf16[32]{0:T(256)(128)(2,1)} %param.27, bf16[128]{0:T(256)(128)(2,1)} %param.29, ...), dimensions={0} | concatenate | bytes 1536 | tf_op jit(solution)/shard_map/concatenate | solution.py:342
  7.3 124.5 %shard_map.271 = (bf16[4,2,2,2,16,128]{5,4,3,2,1,0:T(8,128)(2,1)}, bf16[4,2,2,2,32,3072]{5,4,3,2,1,0:T(8,128)(2,1)}, bf16[4,2,2,2,32,1024]{5,4,3,2,1,0:T(8,128)(...) custom-call(bf16[16,128]{1,0:T(8,128)(2,1)} %pad_bitcast_fusion.1.refs_0_, ...), custom_call_target="tpu_custom_call" | custom-call | tf_op jit(solution)/shard_map/pallas_call | solution.py:161
  131.8 0.9 copy.35
  133.1 1.2 convert_reduce_fusion
  134.3 1.3 fusion.21
  135.6 6.6 %fusion.36 = f32[256,3072]{1,0:T(8,128)} fusion(bf16[1024,3072]{1,0:T(8,128)(2,1)} %bitcast.143, bf16[1,256,1024]{2,1,0:T(8,128)(2,1)} %param.16, f32[1024]{0:T(1024)S(1)} %reshape.416, f32[1024]{0:T(1024)S(1)} %reshape.415, f32[256]{0:T(256)S(1)} %fusion.53, f32[256]{0:T(256)S(1)} %broadcast_multiply_fusion.1), kind=kOutput, calls=%fused_computation.66 | convolution fusion | flops 1612185600 | bytes 9971712 | tf_op jit(solution)/shard_map/dot_general | solution.py:426
  142.3 2.6 fusion.27
  144.9 2.1 slice.126.refs_0_
  147.0 41.1 %shard_map.272 = (bf16[2,2,256,1024]{3,2,1,0:T(8,128)(2,1)}, bf16[2,2,256,1024]{3,2,1,0:T(8,128)(2,1)}) custom-call(bf16[256,1024]{1,0:T(8,128)(2,1)} %slice.126.refs_0_, bf16[256,1024]{1,0:T(8,128)(2,1)} %get-tuple-element.62.refs_1_), custom_call_target="tpu_custom_call" | custom-call | tf_op jit(solution)/shard_map/pallas_call | solution.py:161
  188.2 1.6 fusion.51
  189.9 2.5 copy.31.mask
  192.4 1.6 copy-done.1
  194.0 1.2 copy-done.3
  195.2 12.8 %shard_map.273 = bf16[1,256,1024]{2,1,0:T(8,128)(2,1)S(1)} custom-call(bf16[1,256,1024]{2,1,0:T(8,128)(2,1)S(1)} %get-tuple-element.63.query, bf16[1,1024,1024]{2,1,0:T(8,128)(2,1)S(1)} %bitcast.115, bf16[1,1024,1024]{2,1,0:T(8,128)(2,1)S(1)} %bitcast.117, f32[1,256,1024]{2,1,0:T(8,128)S(1)} %copy-done.3), custom_call_target="tpu_custom_call" | custom-call | tf_op jit(solution)/shard_map/pallas_call | solution.py:494
  208.1 0.8 fusion.64
  209.5 6.0 %convolution_add_fusion = f32[256,4096]{1,0:T(8,128)S(1)} fusion(bf16[1024,4096]{1,0:T(8,128)(2,1)} %bitcast.135, f32[4096]{0:T(1024)S(1)} %fusion.52, f32[256,1024]{1,0:T(8,128)S(1)} %get-tuple-element.83, f32[1024]{0:T(1024)S(1)} %reshape.421, f32[1024]{0:T(1024)S(1)} %reshape.420, f32[256]{0:T(256)S(1)} %fusion.54, f32[256]{0:T(256)S(1)} %broadcast_multiply_fusion), kind=kOutput, calls=%fused_computation.8 | convolution fusion | flops 2149842944 | bytes 13658112 | tf_op jit(solution)/shard_map/dot_general | solution.py:426
  215.5 3.7 fusion.15
  219.2 6.1 %fusion.65 = (bf16[4096]{0:T(1024)(128)(2,1)S(1)}, bf16[256,4096]{1,0:T(8,128)(2,1)S(1)}) fusion(f32[256,4096]{1,0:T(8,128)S(1)} %convolution_add_fusion, bf16[4096,1024]{1,0:T(8,128)(2,1)S(1)} %bitcast.142, bf16[1,256,1024]{2,1,0:T(8,128)(2,1)S(1)} %copy-done.7), kind=kOutput, calls=%fused_computation.114 | convolution fusion | flops 2173693952 | bytes 15212544 | tf_op jit(solution)/shard_map/dot_general | solution.py:436
  225.3 2.7 multiply_reduce_fusion
  228.7 0.9 copy-done.16
  230.3 22.7 %shard_map.274 = (bf16[1,256,1024]{2,1,0:T(8,128)(2,1)S(1)}, bf16[1,1024,1024]{2,1,0:T(8,128)(2,1)S(1)}, bf16[1,1024,1024]{2,1,0:T(8,128)(2,1)}) custom-call(bf16[1,256,1024]{2,1,0:T(8,128)(2,1)S(1)} %get-tuple-element.63.query, bf16[1,1024,1024]{2,1,0:T(8,128)(2,1)} %bitcast.114, bf16[1,1024,1024]{2,1,0:T(8,128)(2,1)} %bitcast.116, ...), custom_call_target="tpu_custom_call" | custom-call | tf_op jit(solution)/shard_map/pallas_call | solution.py:508
  253.0 1.4 copy-done.4
  254.4 40.8 %shard_map.275 = (f32[256,1024]{1,0:T(8,128)S(1)}, f32[256,1024]{1,0:T(8,128)}) custom-call(bf16[2,2,256,1024]{3,2,1,0:T(8,128)(2,1)} %bitcast.118, bf16[2,2,256,1024]{3,2,1,0:T(8,128)(2,1)} %bitcast.128), custom_call_target="tpu_custom_call" | custom-call | tf_op jit(solution)/shard_map/pallas_call | solution.py:313
  295.2 1.3 fusion.61
  296.5 1.0 convert_element_type.209
  297.5 4.9 %fusion.58 = (bf16[1024]{0:T(1024)(128)(2,1)S(1)}, f32[256]{0:T(256)S(1)}, f32[256,1024]{1,0:T(8,128)S(1)}) fusion(f32[1024]{0:T(1024)S(1)} %reshape.415, f32[256]{0:T(256)S(1)} %broadcast_multiply_fusion.1, bf16[1,256,1024]{2,1,0:T(8,128)(2,1)S(1)} %copy-done.6, bf16[1024,3072]{1,0:T(8,128)(2,1)} %bitcast.144, ...), kind=kOutput, calls=%fused_computation.108 | convolution fusion | flops 1616902912 | bytes 9445376 | tf_op jit(solution)/shard_map/dot_general | solution.py:436
  303.0 1.3 fusion.33
  305.3 6.0 %convolution_convert_fusion.2 = bf16[1024,3072]{1,0:T(8,128)(2,1)} fusion(bf16[256,1024]{1,0:T(8,128)(2,1)} %copy-done.13, bf16[256,1024]{1,0:T(8,128)(2,1)} %convert_element_type.209, bf16[256,1024]{1,0:T(8,128)(2,1)S(1)} %bitcast.121, bf16[1,256,1024]{2,1,0:T(8,128)(2,1)S(1)} %copy-done.6, f32[1024]{0:T(1024)S(1)} %reshape.416, f32[256]{0:T(256)S(1)} %fusion.53, ...), kind=kOutput, calls=%fused_computation.6 | convolution fusion | flops 1620049920 | bytes 8398848 | tf_op jit(solution)/shard_map/dot_general | solution.py:430
  311.3 2.1 convolution_convert_fusion.3
  313.4 5.7 %convolution_convert_fusion.1 = bf16[1024,4096]{1,0:T(8,128)(2,1)} fusion(bf16[256,4096]{1,0:T(8,128)(2,1)S(1)} %copy-done.10, f32[256,1024]{1,0:T(8,128)S(1)} %get-tuple-element.83, f32[1024]{0:T(1024)S(1)} %reshape.421, f32[1024]{0:T(1024)S(1)} %reshape.420, f32[256]{0:T(256)S(1)} %fusion.54, f32[256]{0:T(256)S(1)} %broadcast_multiply_fusion), kind=kOutput, calls=%fused_computation.1 | convolution fusion | flops 2152988672 | bytes 11544576 | tf_op jit(solution)/shard_map/dot_general | solution.py:430
  319.2 5.2 %convolution_convert_fusion = bf16[4096,1024]{1,0:T(8,128)(2,1)} fusion(bf16[1,256,1024]{2,1,0:T(8,128)(2,1)S(1)} %copy-done.8, f32[256,4096]{1,0:T(8,128)S(1)} %copy-done.18), kind=kOutput, calls=%fused_computation | convolution fusion | flops 2161115136 | bytes 13107200 | tf_op jit(solution)/shard_map/dot_general | solution.py:430
  324.4 119.8 %shard_map.276 = (f32[16,128]{1,0:T(8,128)S(1)}, f32[32,3072]{1,0:T(8,128)S(1)}, f32[32,1024]{1,0:T(8,128)S(1)}, f32[32,4096]{1,0:T(8,128)S(1)}, f32[128,1024]{1,0:T(8,128)S(1)}) custom-call(bf16[4,2,2,2,16,128]{5,4,3,2,1,0:T(8,128)(2,1)S(1)} %bitcast.119, bf16[4,2,2,2,32,3072]{5,4,3,2,1,0:T(8,128)(2,1)} %bitcast.127, ...), custom_call_target="tpu_custom_call" | custom-call | tf_op jit(solution)/shard_map/pallas_call | solution.py:313
  (89 shorter events, 8.8 us)
Async XLA Ops:
  142.2 46.0 %copy-start.14 = (s32[1,1024]{1,0:T(1,128)S(1)}, s32[1,1024]{1,0:T(1,128)}, u32[]{:S(2)}) copy-start(s32[1,1024]{1,0:T(1,128)} %param.17) | copy-start | bytes 12292
  188.2 4.2 copy-start
  192.4 1.6 copy-start.1
  194.0 1.2 copy-start.3
  195.2 12.8 %copy-start.5 = (bf16[1,256,1024]{2,1,0:T(8,128)(2,1)S(1)}, bf16[1,256,1024]{2,1,0:T(8,128)(2,1)}, u32[]{:S(2)}) copy-start(bf16[1,256,1024]{2,1,0:T(8,128)(2,1)} %param.16) | copy-start | bytes 1572868
  195.2 12.9 %copy-start.15 = (bf16[4,2,2,2,32,1024]{5,4,3,2,1,0:T(8,128)(2,1)S(1)}, bf16[4,2,2,2,32,1024]{5,4,3,2,1,0:T(8,128)(2,1)}, u32[]{:S(2)}) copy-start(bf16[4,2,2,2,32,1024]{5,4,3,2,1,0:T(8,128)(2,1)} %get-tuple-element.36) | copy-start | bytes 6291460
  209.2 6.3 %slice-start.2 = ((s8[8388608]{0:T(1024)(128)(4,1)}), s8[4194304]{0:T(1024)(128)(4,1)S(1)}, s32[]{:S(2)}) async-start(s8[8388608]{0:T(1024)(128)(4,1)} %bitcast.139), calls=%async_computation.2 | async-start | bytes 8388608
  209.5 6.0 %slice-start.3 = ((s8[8388608]{0:T(1024)(128)(4,1)}), s8[4194304]{0:T(1024)(128)(4,1)S(1)}, s32[]{:S(2)}) async-start(s8[8388608]{0:T(1024)(128)(4,1)} %bitcast.139), calls=%async_computation.3 | async-start | bytes 8388608
  215.5 3.7 copy-start.17
  215.5 3.7 copy-start.7
  215.5 9.8 %slice-start = ((s8[8388608]{0:T(1024)(128)(4,1)}), s8[4194304]{0:T(1024)(128)(4,1)S(1)}, s32[]{:S(2)}) async-start(s8[8388608]{0:T(1024)(128)(4,1)} %bitcast.136), calls=%async_computation | async-start | bytes 8388608
  219.2 6.1 %slice-start.1 = ((s8[8388608]{0:T(1024)(128)(4,1)}), s8[4194304]{0:T(1024)(128)(4,1)S(1)}, s32[]{:S(2)}) async-start(s8[8388608]{0:T(1024)(128)(4,1)} %bitcast.136), calls=%async_computation.1 | async-start | bytes 8388608
  225.3 2.7 copy-start.9
  228.0 1.6 copy-start.16
  228.0 2.3 copy-start.2
  228.7 24.3 %copy-start.11 = (bf16[256,1024]{1,0:T(8,128)(2,1)}, bf16[256,1024]{1,0:T(8,128)(2,1)S(1)}, u32[]{:S(2)}) copy-start(bf16[256,1024]{1,0:T(8,128)(2,1)S(1)} %get-tuple-element.57) | copy-start | bytes 1572868
  253.0 1.4 copy-start.4
  254.4 43.1 %copy-start.6 = (bf16[1,256,1024]{2,1,0:T(8,128)(2,1)S(1)}, bf16[1,256,1024]{2,1,0:T(8,128)(2,1)}, u32[]{:S(2)}) copy-start(bf16[1,256,1024]{2,1,0:T(8,128)(2,1)} %param.16) | copy-start | bytes 1572868
  296.5 1.0 copy-start.13
  302.4 2.5 copy-start.8
  305.3 6.0 %copy-start.12 = (bf16[256,1024]{1,0:T(8,128)(2,1)S(1)}, bf16[256,1024]{1,0:T(8,128)(2,1)}, u32[]{:S(2)}) copy-start(bf16[256,1024]{1,0:T(8,128)(2,1)} %copy-done.11) | copy-start | bytes 1572868
  305.3 8.1 %copy-start.10 = (bf16[256,4096]{1,0:T(8,128)(2,1)S(1)}, bf16[256,4096]{1,0:T(8,128)(2,1)}, u32[]{:S(2)}) copy-start(bf16[256,4096]{1,0:T(8,128)(2,1)} %copy-done.9) | copy-start | bytes 6291460
  313.4 5.7 %copy-start.18 = (f32[256,4096]{1,0:T(8,128)S(1)}, f32[256,4096]{1,0:T(8,128)}, u32[]{:S(2)}) copy-start(f32[256,4096]{1,0:T(8,128)} %copy-done.17) | copy-start | bytes 12582916

commit v3 on v2

--- a/solution.py
+++ b/solution.py
@@ -11,7 +11,7 @@
 HEAD_DIM = 64
 
 BLOCK_ROWS = 32
-BLOCK_COLUMNS = 1024
+BLOCK_COLUMNS = 512
 LAG = 2
 MESH = pl.DeviceIdType.MESH
 

time: 451 us -> 441 us (0.978)
  Pallas kernels: 362 us -> 354 us
    pallas_call x2, Pallas kernels: 166 us -> 158 us  [gather_blocks(): pl.pallas_call(functools.partial(gather_kernel, dims, sizes, pieces, coun...]
where the time goes in v3:
time: 441 us; the launch traced here: 440 us
  Pallas kernels  354 us (80%)
  matrix products  50.5 us (11%)
  local copies, waits for them, and re-layouts  23 us (5%)
  other arithmetic  12.2 us (3%)
    pallas_call x2, Pallas kernels, scatter_blocks(): pl.pallas_call(functools.partial(scatter_kernel, dims, sizes, pieces, cou...  160 us
    pallas_call x2, Pallas kernels, gather_blocks(): pl.pallas_call(functools.partial(gather_kernel, dims, sizes, pieces, coun...  158 us
    pallas_call x1, Pallas kernels, attend_back(): pl.pallas_call(attend_back_kernel, grid=(seqs, width // 128), out_shape=[...  22.7 us
    dot_general x4, matrix products, weight_grad(): lax.dot_general(left, right, (((0,), (0,)), ((), ())), preferred_element_...  19.1 us
    dot_general x4, matrix products, rows_product(): return jnp.dot(left, right, preferred_element_type=jnp.float32)  17 us
    dot_general x4, matrix products, input_grad(): lax.dot_general(left, right, (((1,), (1,)), ((), ())), preferred_element_...  14.4 us
    pallas_call x1, Pallas kernels, attend(): pl.pallas_call(attend_kernel, grid=(seqs, width // 128), out_shape=jax.Sh...  12.8 us
    unnamed x53, local copies, waits for them, and re-layouts  9.13 us

profile of v3, /device:TPU:0, one launch (start us, length us, event | category | flops | bytes accessed | tf_op | source)
XLA Modules:
  0.0 440.3 jit_solution(615079180552634786)
XLA Ops:
  0.6 6.1 %concatenate.10 = bf16[384]{0:T(512)(128)(2,1)S(1)} concatenate(bf16[32]{0:T(256)(128)(2,1)} %param.19, bf16[32]{0:T(256)(128)(2,1)} %param.20, bf16[32]{0:T(256)(128)(2,1)} %param.22, bf16[32]{0:T(256)(128)(2,1)} %param.23, bf16[32]{0:T(256)(128)(2,1)} %param.25, bf16[32]{0:T(256)(128)(2,1)} %param.26, bf16[32]{0:T(256)(128)(2,1)} %param.27, bf16[128]{0:T(256)(128)(2,1)} %param.29, ...), dimensions={0} | concatenate | bytes 1536 | tf_op jit(solution)/shard_map/concatenate | solution.py:342
  7.3 116.1 %shard_map.271 = (bf16[4,2,2,2,16,128]{5,4,3,2,1,0:T(8,128)(2,1)}, bf16[4,2,2,2,32,3072]{5,4,3,2,1,0:T(8,128)(2,1)}, bf16[4,2,2,2,32,1024]{5,4,3,2,1,0:T(8,128)(...) custom-call(bf16[16,128]{1,0:T(8,128)(2,1)} %pad_bitcast_fusion.1.refs_0_, ...), custom_call_target="tpu_custom_call" | custom-call | tf_op jit(solution)/shard_map/pallas_call | solution.py:161
  123.5 0.9 copy.35
  124.7 1.2 convert_reduce_fusion
  125.9 1.3 fusion.21
  127.3 6.6 %fusion.36 = f32[256,3072]{1,0:T(8,128)} fusion(bf16[1024,3072]{1,0:T(8,128)(2,1)} %bitcast.143, bf16[1,256,1024]{2,1,0:T(8,128)(2,1)} %param.16, f32[1024]{0:T(1024)S(1)} %reshape.416, f32[1024]{0:T(1024)S(1)} %reshape.415, f32[256]{0:T(256)S(1)} %fusion.53, f32[256]{0:T(256)S(1)} %broadcast_multiply_fusion.1), kind=kOutput, calls=%fused_computation.66 | convolution fusion | flops 1612185600 | bytes 9971712 | tf_op jit(solution)/shard_map/dot_general | solution.py:426
  134.0 2.6 fusion.27
  136.6 2.1 slice.126.refs_0_
  138.7 41.7 %shard_map.272 = (bf16[2,2,256,1024]{3,2,1,0:T(8,128)(2,1)}, bf16[2,2,256,1024]{3,2,1,0:T(8,128)(2,1)}) custom-call(bf16[256,1024]{1,0:T(8,128)(2,1)} %slice.126.refs_0_, bf16[256,1024]{1,0:T(8,128)(2,1)} %get-tuple-element.62.refs_1_), custom_call_target="tpu_custom_call" | custom-call | tf_op jit(solution)/shard_map/pallas_call | solution.py:161
  180.4 1.6 fusion.51
  182.0 2.5 copy.31.mask
  184.6 1.6 copy-done.1
  186.2 1.2 copy-done.3
  187.4 12.8 %shard_map.273 = bf16[1,256,1024]{2,1,0:T(8,128)(2,1)S(1)} custom-call(bf16[1,256,1024]{2,1,0:T(8,128)(2,1)S(1)} %get-tuple-element.63.query, bf16[1,1024,1024]{2,1,0:T(8,128)(2,1)S(1)} %bitcast.115, bf16[1,1024,1024]{2,1,0:T(8,128)(2,1)S(1)} %bitcast.117, f32[1,256,1024]{2,1,0:T(8,128)S(1)} %copy-done.3), custom_call_target="tpu_custom_call" | custom-call | tf_op jit(solution)/shard_map/pallas_call | solution.py:494
  200.3 0.8 fusion.64
  201.6 6.0 %convolution_add_fusion = f32[256,4096]{1,0:T(8,128)S(1)} fusion(bf16[1024,4096]{1,0:T(8,128)(2,1)} %bitcast.135, f32[4096]{0:T(1024)S(1)} %fusion.52, f32[256,1024]{1,0:T(8,128)S(1)} %get-tuple-element.83, f32[1024]{0:T(1024)S(1)} %reshape.421, f32[1024]{0:T(1024)S(1)} %reshape.420, f32[256]{0:T(256)S(1)} %fusion.54, f32[256]{0:T(256)S(1)} %broadcast_multiply_fusion), kind=kOutput, calls=%fused_computation.8 | convolution fusion | flops 2149842944 | bytes 13658112 | tf_op jit(solution)/shard_map/dot_general | solution.py:426
  207.7 3.7 fusion.15
  211.4 6.1 %fusion.65 = (bf16[4096]{0:T(1024)(128)(2,1)S(1)}, bf16[256,4096]{1,0:T(8,128)(2,1)S(1)}) fusion(f32[256,4096]{1,0:T(8,128)S(1)} %convolution_add_fusion, bf16[4096,1024]{1,0:T(8,128)(2,1)S(1)} %bitcast.142, bf16[1,256,1024]{2,1,0:T(8,128)(2,1)S(1)} %copy-done.7), kind=kOutput, calls=%fused_computation.114 | convolution fusion | flops 2173693952 | bytes 15212544 | tf_op jit(solution)/shard_map/dot_general | solution.py:436
  217.5 2.7 multiply_reduce_fusion
  220.8 0.9 copy-done.16
  222.5 22.7 %shard_map.274 = (bf16[1,256,1024]{2,1,0:T(8,128)(2,1)S(1)}, bf16[1,1024,1024]{2,1,0:T(8,128)(2,1)S(1)}, bf16[1,1024,1024]{2,1,0:T(8,128)(2,1)}) custom-call(bf16[1,256,1024]{2,1,0:T(8,128)(2,1)S(1)} %get-tuple-element.63.query, bf16[1,1024,1024]{2,1,0:T(8,128)(2,1)} %bitcast.114, bf16[1,1024,1024]{2,1,0:T(8,128)(2,1)} %bitcast.116, ...), custom_call_target="tpu_custom_call" | custom-call | tf_op jit(solution)/shard_map/pallas_call | solution.py:508
  245.2 1.4 copy-done.4
  246.5 40.1 %shard_map.275 = (f32[256,1024]{1,0:T(8,128)S(1)}, f32[256,1024]{1,0:T(8,128)}) custom-call(bf16[2,2,256,1024]{3,2,1,0:T(8,128)(2,1)} %bitcast.118, bf16[2,2,256,1024]{3,2,1,0:T(8,128)(2,1)} %bitcast.128), custom_call_target="tpu_custom_call" | custom-call | tf_op jit(solution)/shard_map/pallas_call | solution.py:313
  286.6 1.3 fusion.61
  288.0 1.0 convert_element_type.209
  288.9 4.9 %fusion.58 = (bf16[1024]{0:T(1024)(128)(2,1)S(1)}, f32[256]{0:T(256)S(1)}, f32[256,1024]{1,0:T(8,128)S(1)}) fusion(f32[1024]{0:T(1024)S(1)} %reshape.415, f32[256]{0:T(256)S(1)} %broadcast_multiply_fusion.1, bf16[1,256,1024]{2,1,0:T(8,128)(2,1)S(1)} %copy-done.6, bf16[1024,3072]{1,0:T(8,128)(2,1)} %bitcast.144, ...), kind=kOutput, calls=%fused_computation.108 | convolution fusion | flops 1616902912 | bytes 9445376 | tf_op jit(solution)/shard_map/dot_general | solution.py:436
  294.4 1.3 fusion.33
  296.7 6.0 %convolution_convert_fusion.2 = bf16[1024,3072]{1,0:T(8,128)(2,1)} fusion(bf16[256,1024]{1,0:T(8,128)(2,1)} %copy-done.13, bf16[256,1024]{1,0:T(8,128)(2,1)} %convert_element_type.209, bf16[256,1024]{1,0:T(8,128)(2,1)S(1)} %bitcast.121, bf16[1,256,1024]{2,1,0:T(8,128)(2,1)S(1)} %copy-done.6, f32[1024]{0:T(1024)S(1)} %reshape.416, f32[256]{0:T(256)S(1)} %fusion.53, ...), kind=kOutput, calls=%fused_computation.6 | convolution fusion | flops 1620049920 | bytes 8398848 | tf_op jit(solution)/shard_map/dot_general | solution.py:430
  302.7 2.1 convolution_convert_fusion.3
  304.9 5.7 %convolution_convert_fusion.1 = bf16[1024,4096]{1,0:T(8,128)(2,1)} fusion(bf16[256,4096]{1,0:T(8,128)(2,1)S(1)} %copy-done.10, f32[256,1024]{1,0:T(8,128)S(1)} %get-tuple-element.83, f32[1024]{0:T(1024)S(1)} %reshape.421, f32[1024]{0:T(1024)S(1)} %reshape.420, f32[256]{0:T(256)S(1)} %fusion.54, f32[256]{0:T(256)S(1)} %broadcast_multiply_fusion), kind=kOutput, calls=%fused_computation.1 | convolution fusion | flops 2152988672 | bytes 11544576 | tf_op jit(solution)/shard_map/dot_general | solution.py:430
  310.6 5.2 %convolution_convert_fusion = bf16[4096,1024]{1,0:T(8,128)(2,1)} fusion(bf16[1,256,1024]{2,1,0:T(8,128)(2,1)S(1)} %copy-done.8, f32[256,4096]{1,0:T(8,128)S(1)} %copy-done.18), kind=kOutput, calls=%fused_computation | convolution fusion | flops 2161115136 | bytes 13107200 | tf_op jit(solution)/shard_map/dot_general | solution.py:430
  315.8 120.3 %shard_map.276 = (f32[16,128]{1,0:T(8,128)S(1)}, f32[32,3072]{1,0:T(8,128)S(1)}, f32[32,1024]{1,0:T(8,128)S(1)}, f32[32,4096]{1,0:T(8,128)S(1)}, f32[128,1024]{1,0:T(8,128)S(1)}) custom-call(bf16[4,2,2,2,16,128]{5,4,3,2,1,0:T(8,128)(2,1)S(1)} %bitcast.119, bf16[4,2,2,2,32,3072]{5,4,3,2,1,0:T(8,128)(2,1)} %bitcast.127, ...), custom_call_target="tpu_custom_call" | custom-call | tf_op jit(solution)/shard_map/pallas_call | solution.py:313
  (89 shorter events, 8.8 us)
Async XLA Ops:
  133.8 46.5 %copy-start.14 = (s32[1,1024]{1,0:T(1,128)S(1)}, s32[1,1024]{1,0:T(1,128)}, u32[]{:S(2)}) copy-start(s32[1,1024]{1,0:T(1,128)} %param.17) | copy-start | bytes 12292
  180.3 4.2 copy-start
  184.6 1.6 copy-start.1
  186.2 1.2 copy-start.3
  187.4 12.8 %copy-start.5 = (bf16[1,256,1024]{2,1,0:T(8,128)(2,1)S(1)}, bf16[1,256,1024]{2,1,0:T(8,128)(2,1)}, u32[]{:S(2)}) copy-start(bf16[1,256,1024]{2,1,0:T(8,128)(2,1)} %param.16) | copy-start | bytes 1572868
  187.4 12.9 %copy-start.15 = (bf16[4,2,2,2,32,1024]{5,4,3,2,1,0:T(8,128)(2,1)S(1)}, bf16[4,2,2,2,32,1024]{5,4,3,2,1,0:T(8,128)(2,1)}, u32[]{:S(2)}) copy-start(bf16[4,2,2,2,32,1024]{5,4,3,2,1,0:T(8,128)(2,1)} %get-tuple-element.36) | copy-start | bytes 6291460
  201.4 6.3 %slice-start.2 = ((s8[8388608]{0:T(1024)(128)(4,1)}), s8[4194304]{0:T(1024)(128)(4,1)S(1)}, s32[]{:S(2)}) async-start(s8[8388608]{0:T(1024)(128)(4,1)} %bitcast.139), calls=%async_computation.2 | async-start | bytes 8388608
  201.6 6.0 %slice-start.3 = ((s8[8388608]{0:T(1024)(128)(4,1)}), s8[4194304]{0:T(1024)(128)(4,1)S(1)}, s32[]{:S(2)}) async-start(s8[8388608]{0:T(1024)(128)(4,1)} %bitcast.139), calls=%async_computation.3 | async-start | bytes 8388608
  207.7 3.7 copy-start.17
  207.7 3.7 copy-start.7
  207.7 9.8 %slice-start = ((s8[8388608]{0:T(1024)(128)(4,1)}), s8[4194304]{0:T(1024)(128)(4,1)S(1)}, s32[]{:S(2)}) async-start(s8[8388608]{0:T(1024)(128)(4,1)} %bitcast.136), calls=%async_computation | async-start | bytes 8388608
  211.3 6.1 %slice-start.1 = ((s8[8388608]{0:T(1024)(128)(4,1)}), s8[4194304]{0:T(1024)(128)(4,1)S(1)}, s32[]{:S(2)}) async-start(s8[8388608]{0:T(1024)(128)(4,1)} %bitcast.136), calls=%async_computation.1 | async-start | bytes 8388608
  217.4 2.7 copy-start.9
  220.1 1.6 copy-start.16
  220.2 2.3 copy-start.2
  220.8 24.3 %copy-start.11 = (bf16[256,1024]{1,0:T(8,128)(2,1)}, bf16[256,1024]{1,0:T(8,128)(2,1)S(1)}, u32[]{:S(2)}) copy-start(bf16[256,1024]{1,0:T(8,128)(2,1)S(1)} %get-tuple-element.57) | copy-start | bytes 1572868
  245.2 1.4 copy-start.4
  246.5 42.4 %copy-start.6 = (bf16[1,256,1024]{2,1,0:T(8,128)(2,1)S(1)}, bf16[1,256,1024]{2,1,0:T(8,128)(2,1)}, u32[]{:S(2)}) copy-start(bf16[1,256,1024]{2,1,0:T(8,128)(2,1)} %param.16) | copy-start | bytes 1572868
  287.9 1.0 copy-start.13
  293.8 2.5 copy-start.8
  296.7 6.0 %copy-start.12 = (bf16[256,1024]{1,0:T(8,128)(2,1)S(1)}, bf16[256,1024]{1,0:T(8,128)(2,1)}, u32[]{:S(2)}) copy-start(bf16[256,1024]{1,0:T(8,128)(2,1)} %copy-done.11) | copy-start | bytes 1572868
  296.7 8.1 %copy-start.10 = (bf16[256,4096]{1,0:T(8,128)(2,1)S(1)}, bf16[256,4096]{1,0:T(8,128)(2,1)}, u32[]{:S(2)}) copy-start(bf16[256,4096]{1,0:T(8,128)(2,1)} %copy-done.9) | copy-start | bytes 6291460
  304.9 5.7 %copy-start.18 = (f32[256,4096]{1,0:T(8,128)S(1)}, f32[256,4096]{1,0:T(8,128)}, u32[]{:S(2)}) copy-start(f32[256,4096]{1,0:T(8,128)} %copy-done.17) | copy-start | bytes 12582916
